TPU v7x, 512 devices: a whole 4x4x16 slice. The times are simulated.
512 devices in a mesh: row: 64 (over z_lo, y, x), col: 8 (over z_hi, core).
Axes of the slice: x: 4, y: 4, z: 16 (z_hi: 4, z_lo: 4; z = z_hi * 4 + z_lo), core: 2. Of those that a mesh axis runs over, the one named last changes fastest.
Arguments:
- blocks: bfloat16 [128, 256, 256], P('col')
- position: int32 [128], replicated, may hold values from 0 to 15
- primal: bfloat16 [4096, 4096], P('row', 'col'), as said below
- dual_inverse: bfloat16 [4096, 4096], P('row', 'col')
Outputs:
- factor: float32 [128, 16], P('row')
- reduced: float32 [128, 128], P('row', 'col')
Inputs may be any that keep to these rules, and one draw needn't show every extreme that they name: primal, dual_inverse and each block are exactly symmetric.
All inputs are finite; a program needn't handle non-finite values.
Results may differ from a plain program's by a relative error of at most 0.0003.
Values may be sent and summed in bfloat16 or wider, within the bound.
A program may use at most 64 MiB of HBM per device.

v0:
```python
import jax
import jax.numpy as jnp
from jax import lax
from jax.sharding import PartitionSpec as P

BLOCK = 256
PANELS = 2


def from_root(block, axis, owner):
    block = jnp.where(lax.axis_index(axis) == owner, block, jnp.zeros_like(block))
    return lax.psum(block, axis)


def panel_factor(column, low_col, panel_cols):
    diagonal = column[low_col : low_col + panel_cols]
    lower = jnp.linalg.cholesky(diagonal)
    solved = lax.linalg.triangular_solve(
        lower, column, left_side=False, lower=True, transpose_a=True
    )
    before = jnp.zeros((low_col, panel_cols), jnp.float32)
    return jnp.concatenate([before, lower, solved[low_col + panel_cols :]], axis=0)


def on_device(blocks, position, primal, dual_inverse):
    row_count = lax.axis_size("row")
    col_count = lax.axis_size("col")
    tile_cols = blocks.shape[0]
    per_row = tile_cols * col_count // row_count
    row_id = lax.axis_index("row")
    col_id = lax.axis_index("col")
    x_panel, w_panel = (
        lax.all_gather(primal, "row", axis=0, tiled=True),
        lax.all_gather(dual_inverse, "row", axis=0, tiled=True),
    )
    panel_pos = x_panel.shape[1] // BLOCK
    first_row = row_id * per_row
    slot_start = first_row % tile_cols
    holder = first_row // tile_cols
    own_blocks = lax.dynamic_slice_in_dim(blocks, slot_start, per_row, 0)
    row_blocks = from_root(own_blocks, "col", holder)
    row_pos = lax.dynamic_slice_in_dim(position, first_row, per_row, 0)
    col_pos = lax.dynamic_slice_in_dim(position, col_id * tile_cols, tile_cols, 0)

    def take_rows(entry):
        start = entry * BLOCK
        return (
            lax.dynamic_slice_in_dim(x_panel, start, BLOCK, 0),
            lax.dynamic_slice_in_dim(w_panel, start, BLOCK, 0),
        )

    def one_field(operands):
        block, entry = operands
        x_rows, w_rows = take_rows(entry)
        left_prod = jnp.dot(block, w_rows, preferred_element_type=jnp.float32).astype(jnp.bfloat16)
        x_split = x_rows.reshape(BLOCK, panel_pos, BLOCK)
        l_split = left_prod.reshape(BLOCK, panel_pos, BLOCK)
        return jnp.einsum(
            "aqc,aqd->qcd", x_split, l_split, preferred_element_type=jnp.float32
        ).astype(jnp.bfloat16)

    fields = lax.map(one_field, (row_blocks, row_pos))
    gathered = lax.all_gather(fields, "col", axis=1, tiled=True)
    npos_all = gathered.shape[1]
    flat_fields = gathered.reshape(per_row * npos_all, BLOCK * BLOCK)
    flat_blocks = blocks.reshape(tile_cols, BLOCK * BLOCK)
    products = lax.dot_general(
        flat_fields, flat_blocks, (((1,), (1,)), ((), ())), preferred_element_type=jnp.float32
    )
    products = products.reshape(per_row, npos_all, tile_cols)
    chosen = col_pos[None, :] == jnp.arange(npos_all, dtype=jnp.int32)[:, None]
    schur_tile = jnp.sum(jnp.where(chosen[None], products, 0.0), axis=1)
    panel_cols = tile_cols // 2
    factor_list = []
    for panel in range(PANELS):
        low_col = panel * panel_cols
        panel_column = lax.all_gather(
            schur_tile[:, low_col : low_col + panel_cols], "row", axis=0, tiled=True
        )
        factor_full = from_root(panel_factor(panel_column, low_col, panel_cols), "col", 0)
        factor_rows = lax.dynamic_slice_in_dim(factor_full, first_row, per_row, 0)
        factor_cols = lax.dynamic_slice_in_dim(factor_full, col_id * tile_cols, tile_cols, 0)
        schur_tile = schur_tile - jnp.dot(
            factor_rows, factor_cols.T, precision=lax.Precision.HIGHEST
        )
        factor_list.append(factor_rows)
    row_index = first_row + jnp.arange(per_row)
    col_index = col_id * tile_cols + jnp.arange(tile_cols)
    bound = PANELS * panel_cols
    keeper = (row_index[:, None] >= bound) & (col_index[None, :] >= bound)
    reduced = jnp.where(keeper, schur_tile, 0.0)
    return (jnp.concatenate(factor_list, axis=1), reduced)


def solution(mesh):
    in_specs = (P("col", None, None), P(), P("row", "col"), P("row", "col"))
    out_specs = (P("row", None), P("row", "col"))
    return jax.shard_map(
        on_device, mesh=mesh, in_specs=in_specs, out_specs=out_specs, check_vma=False
    )
```

profile of v0, /device:TPU:1, one launch (start us, length us, event | category | flops | bytes accessed | tf_op | source)
XLA Modules:
  0.0 1258.0 jit_solution(8951142634142341959)
XLA Ops:
  8.1 1.7 dynamic-slice_select_fusion
  9.8 0.5 all-gather.6.cloned.1.call-update
  10.4 0.5 all-gather.8.cloned.1.call-update
  11.0 0.7 dynamic_slice.36
  11.7 103.8 %all-reduce.2.cloned.1.call-done = bf16[2,256,256]{2,1,0:T(8,128)(2,1)} async-done(((bf16[2,256,256]{2,1,0:T(8,128)(2,1)}), bf16[2,256,256]{2,1,0:T(8,128)(2,1)}) %all-reduce.2.cloned.1.call-update) | async-done | bytes 262160 | tf_op jit(solution)/shard_map/psum | solution.py:12
  115.6 217.5 %all-gather.6.cloned.1.call-done = bf16[4096,512]{1,0:T(8,128)(2,1)} async-done(((bf16[64,512]{1,0:T(8,128)(2,1)}), bf16[4096,512]{1,0:T(8,128)(2,1)}) %all-gather.6.cloned.1.call-update) | async-done | bytes 4194320 | tf_op jit(solution)/shard_map/all_gather | solution.py:33
  333.0 356.9 %all-gather.8.cloned.1.call-done = bf16[4096,512]{1,0:T(8,128)(2,1)} async-done(((bf16[64,512]{1,0:T(8,128)(2,1)}), bf16[4096,512]{1,0:T(8,128)(2,1)}) %all-gather.8.cloned.1.call-update) | async-done | bytes 4194320 | tf_op jit(solution)/shard_map/all_gather | solution.py:34
  690.0 7.8 while.10
  690.0 0.6 dynamic_slice.63
  691.3 1.3 convolution_convert_fusion.3
  692.5 1.0 constant_dynamic-slice_fusion.4
  693.7 0.2 fusion.50
  693.9 0.6 dynamic_slice.63
  695.2 1.2 convolution_convert_fusion.3
  696.4 1.0 constant_dynamic-slice_fusion.4
  697.8 0.8 copy-done
  698.7 142.9 %all-gather.10.cloned.1.call-done = bf16[2,16,256,256]{3,2,0,1:T(8,128)(2,1)} async-done(((bf16[2,2,256,256]{3,2,0,1:T(8,128)(2,1)}), bf16[2,16,256,256]{3,2,0,1:T(8,128)(2,1)}) %all-gather.10.cloned.1.call-update) | async-done | bytes 4194320 | tf_op jit(solution)/shard_map/all_gather | solution.py:63
  841.6 5.8 fusion.22
  847.4 152.2 %all-gather = f32[64,2,8]{2,1,0:T(2,128)S(1)} all-gather(f32[1,2,8]{2,1,0:T(2,128)S(1)} %slice_bitcast_fusion.1), channel_id=1, replica_groups=mesh['row'=64,'col'=8] {'row'}, dimensions={0}, use_global_device_ids=true | all-gather | bytes 4160 | tf_op jit(solution)/shard_map/all_gather | solution.py:77
  999.6 0.7 cholesky.44
  1000.4 0.6 compare_reduce_fusion.1
  1001.0 0.6 select_bitcast_fusion.1
  1001.7 0.6 custom-call.6
  1002.8 45.0 %psum.22 = f32[128,8]{0,1:T(8,128)S(1)} all-reduce(f32[128,8]{0,1:T(8,128)S(1)} %maximum_select_fusion), channel_id=1, replica_groups=mesh['row'=64,'col'=8] {'col'}, use_global_device_ids=true, to_apply=%region_6.9 | all-reduce | flops 1024 | bytes 8192 | tf_op jit(solution)/shard_map/psum | solution.py:12
  1048.2 151.7 %all-gather.1 = f32[64,2,8]{2,1,0:T(2,128)S(1)} all-gather(f32[1,2,8]{2,1,0:T(2,128)S(1)} %slice_bitcast_fusion), channel_id=1, replica_groups=mesh['row'=64,'col'=8] {'row'}, dimensions={0}, use_global_device_ids=true | all-gather | bytes 4160 | tf_op jit(solution)/shard_map/all_gather | solution.py:77
  1200.0 0.7 cholesky.55
  1200.7 0.6 compare_reduce_fusion
  1201.4 0.6 select_bitcast_fusion
  1202.0 0.6 custom-call.7
  1203.1 45.9 %psum.23 = f32[128,8]{0,1:T(8,128)S(1)} all-reduce(f32[128,8]{0,1:T(8,128)S(1)} %maximum_select_fusion.1), channel_id=1, replica_groups=mesh['row'=64,'col'=8] {'col'}, use_global_device_ids=true, to_apply=%region_7.10 | all-reduce | flops 1024 | bytes 8192 | tf_op jit(solution)/shard_map/psum | solution.py:12
  1249.1 0.8 fusion.27
  1249.9 0.6 pad_maximum_fusion
  (44 shorter events, 2.5 us)
Async XLA Ops:
  8.0 107.6 %all-reduce.2.cloned.1.call-start = ((), (), s32[]{:S(2)}) async-start(), calls=%async_computation.1 | async-start | bytes 524288 | tf_op jit(solution)/shard_map/psum | solution.py:12
  9.8 323.3 %all-gather.6.cloned.1.call-start = ((), (), s32[]{:S(2)}) async-start(), calls=%async_computation | async-start | bytes 4259840 | tf_op jit(solution)/shard_map/all_gather | solution.py:33
  10.4 679.6 %all-gather.8.cloned.1.call-start = ((), (), s32[]{:S(2)}) async-start(), calls=%async_computation.2 | async-start | bytes 4259840 | tf_op jit(solution)/shard_map/all_gather | solution.py:34
  10.9 830.6 %all-gather.10.cloned.1.call-start = ((), (), s32[]{:S(2)}) async-start(), calls=%async_computation.3 | async-start | bytes 4718592 | tf_op jit(solution)/shard_map/all_gather | solution.py:63
  690.0 8.6 copy-start.2
  690.0 151.6 %copy-start.1 = (bf16[16,256,256]{2,1,0:T(8,128)(2,1)S(1)}, bf16[16,256,256]{2,1,0:T(8,128)(2,1)}, u32[]{:S(2)}) copy-start(bf16[16,256,256]{2,1,0:T(8,128)(2,1)} %param.9) | copy-start | bytes 6291460
  697.8 0.8 copy-start
Sparse Core Ops, SparseCore 0:
  11.7 103.8 all-reduce.1
  698.7 142.8 all-gather.9
Sparse Core Ops, SparseCore 1:
  12.5 320.4 all-gather.5
  335.2 354.7 all-gather.7
where the time goes:
time: 1260 us
  waiting for transfers between devices  822 us (65%)
  blocking collectives  395 us (31%)
  between operations  15.6 us (1%)
    all_gather x1, waiting for transfers between devices, on_device(): lax.all_gather(dual_inverse, 'row', axis=0, tiled=True)  357 us
    all_gather x2, blocking collectives, on_device(): lax.all_gather(schur_tile[:, low_col:low_col + panel_cols], 'row', axis=0...  304 us
    all_gather x1, waiting for transfers between devices, on_device(): lax.all_gather(primal, 'row', axis=0, tiled=True)  217 us
    all_gather x1, waiting for transfers between devices, on_device(): gathered = lax.all_gather(fields, 'col', axis=1, tiled=True)  143 us
    psum x1, waiting for transfers between devices, from_root(): return lax.psum(block, axis)  104 us
    psum x2, blocking collectives, from_root(): return lax.psum(block, axis)  90.9 us
  transfers between devices with their start and end apart: 4, of which 4 were waited for; matrix products, arithmetic and copies ran while one was open for 0% of the time, Pallas kernels for 0%

commit v1 on v0

v1 whole, which is shorter than its diff:
```python
import functools

import jax
import jax.numpy as jnp
from jax import lax
from jax.experimental import pallas as pl
from jax.experimental.pallas import tpu as pltpu
from jax.sharding import PartitionSpec as P

BLOCK = 256
PANELS = 2
MESH = pl.DeviceIdType.MESH
PIECES = 2
ROWS = 8 // PIECES


def remote(src, dst, send, recv, dev):
    return pltpu.make_async_remote_copy(
        src_ref=src, dst_ref=dst, send_sem=send, recv_sem=recv, device_id=dev, device_id_type=MESH
    )


def await_bytes(ref, sem):
    pltpu.make_async_copy(ref, ref, sem).wait()


def schur_kernel(
    gt, xt, w4, pos_i, pos_j,
    factor_ref, schur_ref,
    ga, gd, xp, wp, lbuf, rbuf, acc, part, share, rs, zs,
    loc_sem, x_send, x_recv, w_send, w_recv, zr_send, zr_recv, zl_send, zl_recv,
    ya_send, xd_send, ya_recv, xd_recv, cp_sem, sa_send, sd_send, sa_recv, sd_recv, red_send, red_recv,
):
    row = lax.axis_index("row")
    col = lax.axis_index("col")
    zlo, y, x = row // 16, (row // 4) % 4, row % 4
    zhi, core = col // 2, col % 2
    z = zhi * 4 + zlo
    sibling = (row, zhi * 2 + (1 - core))

    def at_z(zz, kk):
        zz = zz % 16
        return ((zz % 4) * 16 + y * 4 + x, (zz // 4) * 2 + kk)

    def at_xy(xx, yy, kk):
        return (zlo * 16 + (yy % 4) * 4 + xx % 4, zhi * 2 + kk)

    def in_plane(m):
        return (x + m % 4) % 4, (y + m // 4) % 4

    barrier = pltpu.get_barrier_semaphore()

    def greet(dev):
        pl.semaphore_signal(barrier, inc=1, device_id=dev, device_id_type=MESH)

    for m in range(1, 16):
        xx, yy = in_plane(m)
        greet(at_xy(xx, yy, core))
        greet(at_xy(xx, yy, 1 - core))
        greet(at_z(z + m, core))
    greet(sibling)
    pl.semaphore_wait(barrier, 46)

    def cols(h):
        return pl.ds(((h % 4) * 2 + core) * 16, 16)

    right, left = at_z(z + 1, core), at_z(z + 15, core)

    def right_rows(idx):
        return (idx % (2 * PIECES)) * ROWS

    def left_rows(idx):
        return ((idx + PIECES) % (2 * PIECES)) * ROWS

    base = 64 * x + 16 * y

    @pl.when(zlo == 3)
    def _():
        for idx in range(2 * PIECES):
            t = right_rows(idx)
            remote(gt.at[pl.ds(base + t, ROWS)], ga.at[pl.ds(16 * y + t, ROWS), cols(zhi)],
                   zr_send, zr_recv.at[idx], right).start()

    @pl.when(zlo == 0)
    def _():
        for idx in range(2 * PIECES):
            t = left_rows(idx)
            remote(gt.at[pl.ds(base + t, ROWS)], ga.at[pl.ds(16 * y + t, ROWS), cols(zhi)],
                   zl_send, zl_recv.at[idx], left).start()

    for m in range(1, 4):
        remote(xt, xp.at[y], x_send, x_recv, at_xy(x, y + m, core)).start()
    for m in range(1, 16):
        xx, yy = in_plane(m)
        remote(w4.at[yy], wp.at[y * 4 + x], w_send, w_recv, at_xy(xx, yy, core)).start()
    pltpu.make_async_copy(xt, xp.at[y], loc_sem.at[0]).start()
    pltpu.make_async_copy(w4.at[y], wp.at[y * 4 + x], loc_sem.at[1]).start()

    own_a = gt.at[pl.ds(64 * x, 64)]
    pltpu.make_async_copy(own_a, ga.at[:, cols(zhi)], loc_sem.at[2]).start()
    remote(own_a, ga.at[:, cols(zhi)], sa_send.at[3], sa_recv.at[3], sibling).start()
    for s in range(4):
        own_d = gt.at[pl.ds(64 * s + 16 * y, 16)]
        pltpu.make_async_copy(own_d, gd.at[pl.ds(16 * s, 16), cols(zhi)], loc_sem.at[3]).start()
        remote(own_d, gd.at[pl.ds(16 * s, 16), cols(zhi)], sd_send.at[3], sd_recv.at[3], sibling).start()

    def spread(t, h, item):
        a_part = ga.at[pl.ds(16 * y + t, ROWS), cols(h)]
        d_part = gd.at[pl.ds(16 * x + t, ROWS), cols(h)]
        for m in range(1, 4):
            remote(a_part, a_part, ya_send.at[item], ya_recv.at[item], at_xy(x, y + m, core)).start()
            remote(a_part, d_part, xd_send.at[item], xd_recv.at[item], at_xy(x + m, y, core)).start()
        pltpu.make_async_copy(a_part, d_part, cp_sem.at[item]).start()

    def hand_over(h, item):
        await_bytes(ga.at[pl.ds(0, 48), pl.ds(0, 16)], ya_recv.at[item])
        part_a = ga.at[:, cols(h)]
        remote(part_a, part_a, sa_send.at[item], sa_recv.at[item], sibling).start()
        await_bytes(ga.at[pl.ds(0, 48), pl.ds(0, 16)], xd_recv.at[item])
        await_bytes(ga.at[pl.ds(0, 16), pl.ds(0, 16)], cp_sem.at[item])
        part_d = gd.at[:, cols(h)]
        remote(part_d, part_d, sd_send.at[item], sd_recv.at[item], sibling).start()

    for idx in range(3 * PIECES):
        first = idx < 2 * PIECES
        h = zhi + 3 if first else zhi + 2
        t = right_rows(idx)
        a_part = ga.at[pl.ds(16 * y + t, ROWS), cols(h)]
        await_bytes(a_part, zr_recv.at[idx])

        @pl.when(zlo < 3)
        def _():
            remote(a_part, a_part, zr_send, zr_recv.at[idx], right).start()

        if idx < PIECES:
            @pl.when(zlo == 3)
            def _():
                remote(a_part, a_part, zr_send, zr_recv.at[idx + 2 * PIECES], right).start()

        h2 = zhi + 1 if first else zhi + 2
        t2 = left_rows(idx)
        b_part = ga.at[pl.ds(16 * y + t2, ROWS), cols(h2)]
        await_bytes(b_part, zl_recv.at[idx])

        @pl.when(zlo > 0)
        def _():
            remote(b_part, b_part, zl_send, zl_recv.at[idx], left).start()

        if idx < PIECES:
            @pl.when(zlo == 0)
            def _():
                remote(b_part, b_part, zl_send, zl_recv.at[idx + 2 * PIECES], left).start()

        spread(t, h, 0 if first else 2)
        spread(t2, h2, 1 if first else 2)

    hand_over(zhi + 3, 0)
    hand_over(zhi + 1, 1)
    hand_over(zhi + 2, 2)

    pltpu.make_async_copy(xt, xp.at[y], loc_sem.at[0]).wait()
    pltpu.make_async_copy(w4.at[y], wp.at[y * 4 + x], loc_sem.at[1]).wait()
    pltpu.make_async_copy(own_a, ga.at[:, cols(zhi)], loc_sem.at[2]).wait()
    await_bytes(gd.at[:, pl.ds(0, 16)], loc_sem.at[3])
    await_bytes(xp.at[pl.ds(0, 3)], x_recv)
    await_bytes(wp.at[pl.ds(0, 15)], w_recv)
    for item in range(4):
        await_bytes(ga.at[:, pl.ds(0, 16)], sa_recv.at[item])
        await_bytes(gd.at[:, pl.ds(0, 16)], sd_recv.at[item])

    weights = jnp.concatenate(
        [wp[4 * p : 4 * p + 4].reshape(BLOCK, 128) for p in range(4)], axis=1
    )
    at_p = [pos_i[...] == 4 * zlo + p for p in range(4)]

    def pick(values, copies):
        total = None
        for p in range(4):
            mask = jnp.concatenate([at_p[p]] * copies, axis=0) if copies > 1 else at_p[p]
            term = jnp.where(mask, values[:, 128 * p : 128 * p + 128], 0.0)
            total = term if total is None else total + term
        return total

    @pl.loop(0, 64, step=4)
    def _(a):
        g = ga[pl.ds(a, 4)].reshape(512, BLOCK)
        full = jnp.dot(g, weights, preferred_element_type=jnp.float32)
        for s in range(4):
            lbuf[a + s] = pick(full[128 * s : 128 * s + 128], 1).astype(jnp.bfloat16)

    xq = [xp[:, :, BLOCK * q : BLOCK * q + BLOCK].reshape(256, BLOCK) for q in range(2)]
    at_q = [pos_j[...] == 2 * col + q for q in range(2)]

    @pl.loop(0, 64, step=2)
    def _(d):
        g = gd[pl.ds(d, 2)].reshape(256, BLOCK)
        for q in range(2):
            full = lax.dot_general(
                xq[q], g, (((1,), (1,)), ((), ())), preferred_element_type=jnp.float32
            )
            for s in range(2):
                start = pl.multiple_of((q * 64 + d + s) * 256, 256)
                rbuf[pl.ds(start, 256)] = jnp.where(at_q[q], full[:, 128 * s : 128 * s + 128], 0.0)

    acc[...] = jnp.zeros_like(acc)

    @pl.loop(0, 64, step=2)
    def _(a):
        lcat = jnp.concatenate([lbuf[a], lbuf[a + 1]], axis=1)
        rows = []
        for s in range(2):
            for q in range(2):
                rows.append(jnp.concatenate(
                    [rbuf[pl.ds(q * 64 * 256 + p * 64 + a + s, 64, stride=256)] for p in range(4)],
                    axis=1,
                ))
        rcat = jnp.concatenate(rows, axis=0).astype(jnp.bfloat16)
        acc[...] += jnp.dot(lcat, rcat, preferred_element_type=jnp.float32)

    part[...] = pick(acc[...], 1)

    me = y * 4 + x
    mine = pl.ds(pl.multiple_of(8 * me, 8), 8)
    for m in range(16):
        xx, yy = in_plane(m)
        theirs = part.at[pl.ds(8 * (yy * 4 + xx), 8)]
        if m:
            remote(theirs, rs.at[core * 16 + me], red_send.at[0], red_recv.at[0], at_xy(xx, yy, core)).start()
        remote(theirs, rs.at[core * 16 + me], red_send.at[0], red_recv.at[0], at_xy(xx, yy, 1 - core)).start()
    rs[core * 16 + me] = part[mine]
    await_bytes(rs.at[pl.ds(0, 31)], red_recv.at[0])
    share[...] = jnp.sum(rs[...], axis=0)
    for m in range(1, 16):
        remote(share, zs.at[z], red_send.at[1], red_recv.at[1], at_z(z + m, core)).start()
    zs[z] = share[...]
    await_bytes(zs.at[pl.ds(0, 15)], red_recv.at[1])
    await_bytes(rs.at[pl.ds(0, 31)], red_send.at[0])
    await_bytes(zs.at[pl.ds(0, 15)], red_send.at[1])
    share[...] = jnp.sum(zs[...], axis=0)
    whole = acc.at[:, pl.ds(0, 128)]
    for m in range(1, 16):
        xx, yy = in_plane(m)
        remote(share, whole.at[mine], red_send.at[2], red_recv.at[2], at_xy(xx, yy, core)).start()
    whole[mine] = share[...]
    await_bytes(zs.at[pl.ds(0, 15)], red_recv.at[2])
    await_bytes(zs.at[pl.ds(0, 15)], red_send.at[2])

    rows = lax.broadcasted_iota(jnp.int32, (128, 128), 0)
    lanes = lax.broadcasted_iota(jnp.int32, (128, 128), 1)
    schur = whole[...]
    factor = jnp.zeros((128, 128), jnp.float32)
    width = 8
    for k in range(PANELS * width):
        lo = k // width * width
        if k == lo:
            inside = (rows >= lo) & (rows < lo + width) & (lanes >= lo) & (lanes < lo + width)
            schur = jnp.where(inside, 0.5 * (schur + schur.T), schur)
        column = jnp.sum(jnp.where(lanes == k, schur, 0.0), axis=1, keepdims=True)
        pivot = jnp.sum(jnp.where(rows[:, :1] == k, column, 0.0), axis=0, keepdims=True)
        column = jnp.where(rows[:, :1] >= k, column / jnp.sqrt(pivot), 0.0)
        line = jnp.sum(jnp.where(rows == lanes, column, 0.0), axis=0, keepdims=True)
        schur = schur - column * line
        factor = jnp.where(lanes == k, column, factor)
    factor_ref[...] = factor
    bound = PANELS * width
    schur_ref[...] = jnp.where((rows >= bound) & (lanes >= bound), schur, 0.0)

    await_bytes(xp.at[pl.ds(0, 3)], x_send)
    await_bytes(wp.at[pl.ds(0, 15)], w_send)
    z_bytes = ga.at[pl.ds(0, 3 * PIECES * ROWS), pl.ds(0, 16)]
    await_bytes(z_bytes, zr_send)
    await_bytes(z_bytes, zl_send)
    for item in range(3):
        await_bytes(ga.at[pl.ds(0, 48), pl.ds(0, 16)], ya_send.at[item])
        await_bytes(ga.at[pl.ds(0, 48), pl.ds(0, 16)], xd_send.at[item])
    for item in range(4):
        await_bytes(ga.at[:, pl.ds(0, 16)], sa_send.at[item])
        await_bytes(gd.at[:, pl.ds(0, 16)], sd_send.at[item])


def on_device(blocks, position, primal, dual_inverse):
    tile_cols = blocks.shape[0]
    rows, width = primal.shape
    row_id = lax.axis_index("row")
    col_id = lax.axis_index("col")
    per_row = tile_cols * lax.axis_size("col") // lax.axis_size("row")
    count = position.shape[0]
    gt = jnp.swapaxes(blocks, 0, 1)
    w4 = dual_inverse.reshape(rows, 2, 4, 4, 16).transpose(3, 0, 1, 2, 4).reshape(4, rows, 128)
    vmem = pl.BlockSpec(memory_space=pltpu.VMEM)
    hbm = pl.BlockSpec(memory_space=pl.ANY)
    bf, f32 = jnp.bfloat16, jnp.float32
    dma = pltpu.SemaphoreType.DMA
    square = jax.ShapeDtypeStruct((count, count), f32)
    factor, schur = pl.pallas_call(
        schur_kernel,
        out_shape=(square, square),
        in_specs=[hbm, vmem, vmem, vmem, vmem],
        out_specs=(vmem, vmem),
        scratch_shapes=[
            pltpu.VMEM((64, count, BLOCK), bf),
            pltpu.VMEM((64, count, BLOCK), bf),
            pltpu.VMEM((4, rows, width), bf),
            pltpu.VMEM((16, rows, 128), bf),
            pltpu.VMEM((64, count, 128), bf),
            pltpu.VMEM((2 * 64 * 256, 128), f32),
            pltpu.VMEM((count, 512), f32),
            pltpu.VMEM((count, count), f32),
            pltpu.VMEM((8, count), f32),
            pltpu.VMEM((32, 8, count), f32),
            pltpu.VMEM((16, 8, count), f32),
            dma((4,)), dma, dma, dma, dma,
            dma, dma((3 * PIECES,)), dma, dma((3 * PIECES,)),
            dma((3,)), dma((3,)), dma((3,)), dma((3,)), dma((3,)), dma((4,)), dma((4,)), dma((4,)), dma((4,)), dma((3,)), dma((3,)),
        ],
        compiler_params=pltpu.CompilerParams(
            collective_id=0, has_side_effects=True, vmem_limit_bytes=56 << 20
        ),
        name="schur",
    )(gt, primal, w4, position.reshape(count, 1), position.reshape(1, count))
    factor_rows = lax.dynamic_slice(factor, (row_id * per_row, 0), (per_row, PANELS * 8))
    reduced = lax.dynamic_slice(schur, (row_id * per_row, col_id * tile_cols), (per_row, tile_cols))
    return factor_rows, reduced


def solution(mesh):
    in_specs = (P("col", None, None), P(), P("row", "col"), P("row", "col"))
    out_specs = (P("row", None), P("row", "col"))
    return jax.shard_map(
        on_device, mesh=mesh, in_specs=in_specs, out_specs=out_specs, check_vma=False
    )
```

time: 1260 us -> 197 us (0.16)
  waiting for transfers between devices: 822 us -> 0 us
  blocking collectives: 395 us -> 0 us
  Pallas kernels: 0 us -> 188 us
  between operations: 15.6 us -> 0.68 us
    all_gather x3 -> x0, waiting for transfers between devices: 717 us -> none  [the longest x1 357 us: on_device(): lax.all_gather(dual_inverse, 'row', axis=0, tiled=True)]
    all_gather x2 -> x0, blocking collectives: 304 us -> none  [on_device(): lax.all_gather(schur_tile[:, low_col:low_col + panel_cols], 'row', axis=0...]
    pallas_call x0 -> x1, Pallas kernels: none -> 188 us  [on_device(): pl.pallas_call(schur_kernel, out_shape=(square, square), in_specs=[hbm, v...]
    psum x1 -> x0, waiting for transfers between devices: 104 us -> none  [from_root(): return lax.psum(block, axis)]
    psum x2 -> x0, blocking collectives: 90.9 us -> none  [from_root(): return lax.psum(block, axis)]
  transfers between devices with their start and end apart: 4 -> 0, of which waited for: 4 -> 0; matrix products, arithmetic and copies ran while one was open for 0% -> 0% of each run, Pallas kernels for 0% -> 0%
where the time goes in v1:
time: 197 us
  Pallas kernels  188 us (95%)
  local copies, waits for them, and re-layouts  8.28 us (4%)
    pallas_call x1, Pallas kernels, on_device(): pl.pallas_call(schur_kernel, out_shape=(square, square), in_specs=[hbm, v...  188 us
    unnamed x6, local copies, waits for them, and re-layouts  4.26 us

profile of v1, /device:TPU:1, one launch (start us, length us, event | category | flops | bytes accessed | tf_op | source)
XLA Modules:
  0.0 197.0 jit_solution(12423242920357033375)
XLA Ops:
  0.6 0.0 copy-start
  0.6 0.0 copy-start.1
  0.7 4.1 %copy.15 = bf16[16,256,256]{2,0,1:T(8,128)(2,1)} copy(bf16[16,256,256]{2,1,0:T(8,128)(2,1)} %param.4) | data formatting | bytes 4194304 | tf_op args[0]
  4.8 0.0 copy-done
  4.8 0.1 copy.10
  4.9 0.7 copy.12.w4
  5.7 0.0 copy-done.1
  5.7 0.7 copy.13.pos_i
  6.4 188.1 %schur.1 = (f32[128,128]{1,0:T(8,128)}, f32[128,128]{1,0:T(8,128)}) custom-call(bf16[256,16,256]{2,1,0:T(8,128)(2,1)} %bitcast.9, bf16[64,512]{1,0:T(8,128)(2,1)} %xt.1, bf16[4,64,128]{2,1,0:T(8,128)(2,1)} %copy.12.w4, s32[128,1]{1,0:T(8,128)} %copy.13.pos_i, s32[1,128]{1,0:T(1,128)} %bitcast.12), custom_call_target="tpu_custom_call" | custom-call | tf_op jit(solution)/shard_map/schur/pallas_call | solution.py:295
  194.5 1.2 constant_dynamic-slice_fusion
  195.7 1.3 dynamic_slice.7
  (1 shorter events, 0.0 us)
Async XLA Ops:
  0.6 4.2 %copy-start = (bf16[64,512]{1,0:T(8,128)(2,1)S(1)}, bf16[64,512]{1,0:T(8,128)(2,1)}, u32[]{:S(2)}) copy-start(bf16[64,512]{1,0:T(8,128)(2,1)} %param.7) | copy-start | bytes 196612
  0.6 5.0 %copy-start.1 = (s32[128]{0:T(128)S(1)}, s32[128]{0:T(128)}, u32[]{:S(2)}) copy-start(s32[128]{0:T(128)} %param.5) | copy-start | bytes 1540

commit v2 on v1

--- a/solution.py
+++ b/solution.py
@@ -10,8 +10,8 @@
 BLOCK = 256
 PANELS = 2
 MESH = pl.DeviceIdType.MESH
-PIECES = 2
-ROWS = 8 // PIECES
+ITEMS = (1, 3, 2)
+PITCH = 264
 
 
 def remote(src, dst, send, recv, dev):
@@ -28,7 +28,7 @@
     gt, xt, w4, pos_i, pos_j,
     factor_ref, schur_ref,
     ga, gd, xp, wp, lbuf, rbuf, acc, part, share, rs, zs,
-    loc_sem, x_send, x_recv, w_send, w_recv, zr_send, zr_recv, zl_send, zl_recv,
+    loc_sem, x_send, x_recv, w_send, w_recv, z_send, z_recv, v_send, v_recv,
     ya_send, xd_send, ya_recv, xd_recv, cp_sem, sa_send, sd_send, sa_recv, sd_recv, red_send, red_recv,
 ):
     row = lax.axis_index("row")
@@ -64,29 +64,18 @@
     def cols(h):
         return pl.ds(((h % 4) * 2 + core) * 16, 16)
 
-    right, left = at_z(z + 1, core), at_z(z + 15, core)
-
-    def right_rows(idx):
-        return (idx % (2 * PIECES)) * ROWS
-
-    def left_rows(idx):
-        return ((idx + PIECES) % (2 * PIECES)) * ROWS
-
     base = 64 * x + 16 * y
-
-    @pl.when(zlo == 3)
-    def _():
-        for idx in range(2 * PIECES):
-            t = right_rows(idx)
-            remote(gt.at[pl.ds(base + t, ROWS)], ga.at[pl.ds(16 * y + t, ROWS), cols(zhi)],
-                   zr_send, zr_recv.at[idx], right).start()
-
-    @pl.when(zlo == 0)
-    def _():
-        for idx in range(2 * PIECES):
-            t = left_rows(idx)
-            remote(gt.at[pl.ds(base + t, ROWS)], ga.at[pl.ds(16 * y + t, ROWS), cols(zhi)],
-                   zl_send, zl_recv.at[idx], left).start()
+    quarter = 4 * zlo
+
+    def share_rows(t, h):
+        return (
+            ga.at[pl.ds(16 * y + t, 4), cols(h)],
+            gd.at[pl.ds(16 * x + t, 4), cols(h)],
+        )
+
+    for item in ITEMS:
+        remote(gt.at[pl.ds(base + quarter, 4)], ga.at[pl.ds(16 * y + quarter, 4), cols(zhi)],
+               z_send.at[item], z_recv.at[item], at_z(z + 4 * item, core)).start()
 
     for m in range(1, 4):
         remote(xt, xp.at[y], x_send, x_recv, at_xy(x, y + m, core)).start()
@@ -98,65 +87,42 @@
 
     own_a = gt.at[pl.ds(64 * x, 64)]
     pltpu.make_async_copy(own_a, ga.at[:, cols(zhi)], loc_sem.at[2]).start()
-    remote(own_a, ga.at[:, cols(zhi)], sa_send.at[3], sa_recv.at[3], sibling).start()
+    remote(own_a, ga.at[:, cols(zhi)], sa_send.at[0], sa_recv.at[0], sibling).start()
     for s in range(4):
         own_d = gt.at[pl.ds(64 * s + 16 * y, 16)]
         pltpu.make_async_copy(own_d, gd.at[pl.ds(16 * s, 16), cols(zhi)], loc_sem.at[3]).start()
-        remote(own_d, gd.at[pl.ds(16 * s, 16), cols(zhi)], sd_send.at[3], sd_recv.at[3], sibling).start()
-
-    def spread(t, h, item):
-        a_part = ga.at[pl.ds(16 * y + t, ROWS), cols(h)]
-        d_part = gd.at[pl.ds(16 * x + t, ROWS), cols(h)]
+        remote(own_d, gd.at[pl.ds(16 * s, 16), cols(zhi)], sd_send.at[0], sd_recv.at[0], sibling).start()
+
+    def spread(t, item):
+        a_part, d_part = share_rows(t, zhi + 4 - item)
         for m in range(1, 4):
             remote(a_part, a_part, ya_send.at[item], ya_recv.at[item], at_xy(x, y + m, core)).start()
             remote(a_part, d_part, xd_send.at[item], xd_recv.at[item], at_xy(x + m, y, core)).start()
         pltpu.make_async_copy(a_part, d_part, cp_sem.at[item]).start()
 
-    def hand_over(h, item):
+    def hand_over(item):
         await_bytes(ga.at[pl.ds(0, 48), pl.ds(0, 16)], ya_recv.at[item])
-        part_a = ga.at[:, cols(h)]
+        part_a = ga.at[:, cols(zhi + 4 - item)]
         remote(part_a, part_a, sa_send.at[item], sa_recv.at[item], sibling).start()
         await_bytes(ga.at[pl.ds(0, 48), pl.ds(0, 16)], xd_recv.at[item])
         await_bytes(ga.at[pl.ds(0, 16), pl.ds(0, 16)], cp_sem.at[item])
-        part_d = gd.at[:, cols(h)]
+        part_d = gd.at[:, cols(zhi + 4 - item)]
         remote(part_d, part_d, sd_send.at[item], sd_recv.at[item], sibling).start()
 
-    for idx in range(3 * PIECES):
-        first = idx < 2 * PIECES
-        h = zhi + 3 if first else zhi + 2
-        t = right_rows(idx)
-        a_part = ga.at[pl.ds(16 * y + t, ROWS), cols(h)]
-        await_bytes(a_part, zr_recv.at[idx])
-
-        @pl.when(zlo < 3)
-        def _():
-            remote(a_part, a_part, zr_send, zr_recv.at[idx], right).start()
-
-        if idx < PIECES:
-            @pl.when(zlo == 3)
-            def _():
-                remote(a_part, a_part, zr_send, zr_recv.at[idx + 2 * PIECES], right).start()
-
-        h2 = zhi + 1 if first else zhi + 2
-        t2 = left_rows(idx)
-        b_part = ga.at[pl.ds(16 * y + t2, ROWS), cols(h2)]
-        await_bytes(b_part, zl_recv.at[idx])
-
-        @pl.when(zlo > 0)
-        def _():
-            remote(b_part, b_part, zl_send, zl_recv.at[idx], left).start()
-
-        if idx < PIECES:
-            @pl.when(zlo == 0)
-            def _():
-                remote(b_part, b_part, zl_send, zl_recv.at[idx + 2 * PIECES], left).start()
-
-        spread(t, h, 0 if first else 2)
-        spread(t2, h2, 1 if first else 2)
-
-    hand_over(zhi + 3, 0)
-    hand_over(zhi + 1, 1)
-    hand_over(zhi + 2, 2)
+    for item in ITEMS:
+        a_part, _ = share_rows(quarter, zhi + 4 - item)
+        await_bytes(a_part, z_recv.at[item])
+        for m in range(1, 4):
+            plane = zhi * 4 + (zlo + m) % 4
+            remote(a_part, a_part, v_send.at[item], v_recv.at[item, m], at_z(plane, core)).start()
+        spread(quarter, item)
+    for item in ITEMS:
+        for m in range(1, 4):
+            t = 4 * ((zlo + 4 - m) % 4)
+            await_bytes(share_rows(t, zhi)[0], v_recv.at[item, m])
+            spread(t, item)
+    for item in ITEMS:
+        hand_over(item)
 
     pltpu.make_async_copy(xt, xp.at[y], loc_sem.at[0]).wait()
     pltpu.make_async_copy(w4.at[y], wp.at[y * 4 + x], loc_sem.at[1]).wait()
@@ -199,22 +165,22 @@
                 xq[q], g, (((1,), (1,)), ((), ())), preferred_element_type=jnp.float32
             )
             for s in range(2):
-                start = pl.multiple_of((q * 64 + d + s) * 256, 256)
+                start = pl.multiple_of((q * 64 + d + s) * PITCH, 8)
                 rbuf[pl.ds(start, 256)] = jnp.where(at_q[q], full[:, 128 * s : 128 * s + 128], 0.0)
 
     acc[...] = jnp.zeros_like(acc)
 
-    @pl.loop(0, 64, step=2)
+    @pl.loop(0, 64, step=4)
     def _(a):
-        lcat = jnp.concatenate([lbuf[a], lbuf[a + 1]], axis=1)
+        lcat = jnp.concatenate([lbuf[a + s] for s in range(4)], axis=1)
         rows = []
-        for s in range(2):
+        for s in range(4):
             for q in range(2):
                 rows.append(jnp.concatenate(
-                    [rbuf[pl.ds(q * 64 * 256 + p * 64 + a + s, 64, stride=256)] for p in range(4)],
+                    [rbuf[pl.ds(q * 64 * PITCH + p * 64 + a + s, 64, stride=PITCH)] for p in range(4)],
                     axis=1,
-                ))
-        rcat = jnp.concatenate(rows, axis=0).astype(jnp.bfloat16)
+                ).astype(jnp.bfloat16))
+        rcat = jnp.concatenate(rows, axis=0)
         acc[...] += jnp.dot(lcat, rcat, preferred_element_type=jnp.float32)
 
     part[...] = pick(acc[...], 1)
@@ -267,10 +233,9 @@
 
     await_bytes(xp.at[pl.ds(0, 3)], x_send)
     await_bytes(wp.at[pl.ds(0, 15)], w_send)
-    z_bytes = ga.at[pl.ds(0, 3 * PIECES * ROWS), pl.ds(0, 16)]
-    await_bytes(z_bytes, zr_send)
-    await_bytes(z_bytes, zl_send)
-    for item in range(3):
+    for item in ITEMS:
+        await_bytes(ga.at[pl.ds(0, 4), pl.ds(0, 16)], z_send.at[item])
+        await_bytes(ga.at[pl.ds(0, 12), pl.ds(0, 16)], v_send.at[item])
         await_bytes(ga.at[pl.ds(0, 48), pl.ds(0, 16)], ya_send.at[item])
         await_bytes(ga.at[pl.ds(0, 48), pl.ds(0, 16)], xd_send.at[item])
     for item in range(4):
@@ -303,15 +268,15 @@
             pltpu.VMEM((4, rows, width), bf),
             pltpu.VMEM((16, rows, 128), bf),
             pltpu.VMEM((64, count, 128), bf),
-            pltpu.VMEM((2 * 64 * 256, 128), f32),
+            pltpu.VMEM((2 * 64 * PITCH, 128), f32),
             pltpu.VMEM((count, 512), f32),
             pltpu.VMEM((count, count), f32),
             pltpu.VMEM((8, count), f32),
             pltpu.VMEM((32, 8, count), f32),
             pltpu.VMEM((16, 8, count), f32),
             dma((4,)), dma, dma, dma, dma,
-            dma, dma((3 * PIECES,)), dma, dma((3 * PIECES,)),
-            dma((3,)), dma((3,)), dma((3,)), dma((3,)), dma((3,)), dma((4,)), dma((4,)), dma((4,)), dma((4,)), dma((3,)), dma((3,)),
+            dma((4,)), dma((4,)), dma((4,)), dma((4, 4)),
+            dma((4,)), dma((4,)), dma((4,)), dma((4,)), dma((4,)), dma((4,)), dma((4,)), dma((4,)), dma((4,)), dma((3,)), dma((3,)),
         ],
         compiler_params=pltpu.CompilerParams(
             collective_id=0, has_side_effects=True, vmem_limit_bytes=56 << 20

time: 197 us -> 97 us (0.49)
  Pallas kernels: 188 us -> 87.3 us
    pallas_call x1, Pallas kernels: 188 us -> 87.3 us  [on_device(): pl.pallas_call(schur_kernel, out_shape=(square, square), in_specs=[hbm, v...]
where the time goes in v2:
time: 97 us; the launch traced here: 96.3 us
  Pallas kernels  87.3 us (90%)
  local copies, waits for them, and re-layouts  8.28 us (9%)
    pallas_call x1, Pallas kernels, on_device(): pl.pallas_call(schur_kernel, out_shape=(square, square), in_specs=[hbm, v...  87.3 us
    unnamed x6, local copies, waits for them, and re-layouts  4.26 us

profile of v2, /device:TPU:1, one launch (start us, length us, event | category | flops | bytes accessed | tf_op | source)
XLA Modules:
  0.0 96.3 jit_solution(15848652437297558315)
XLA Ops:
  0.6 0.0 copy-start
  0.6 0.0 copy-start.1
  0.7 4.1 %copy.15 = bf16[16,256,256]{2,0,1:T(8,128)(2,1)} copy(bf16[16,256,256]{2,1,0:T(8,128)(2,1)} %param.4) | data formatting | bytes 4194304 | tf_op args[0]
  4.8 0.0 copy-done
  4.8 0.1 copy.10
  4.9 0.7 copy.12.w4
  5.7 0.0 copy-done.1
  5.7 0.7 copy.13.pos_i
  6.4 87.3 %schur.1 = (f32[128,128]{1,0:T(8,128)}, f32[128,128]{1,0:T(8,128)}) custom-call(bf16[256,16,256]{2,1,0:T(8,128)(2,1)} %bitcast.9, bf16[64,512]{1,0:T(8,128)(2,1)} %xt.1, bf16[4,64,128]{2,1,0:T(8,128)(2,1)} %copy.12.w4, s32[128,1]{1,0:T(8,128)} %copy.13.pos_i, s32[1,128]{1,0:T(1,128)} %bitcast.12), custom_call_target="tpu_custom_call" | custom-call | tf_op jit(solution)/shard_map/schur/pallas_call | solution.py:260
  93.7 1.2 %constant_dynamic-slice_fusion = f32[2,16]{1,0:T(2,128)} fusion(f32[128,128]{1,0:T(8,128)} %get-tuple-element.4, s32[]{:T(128)S(6)} %select_n.7), kind=kLoop, calls=%fused_computation.1 | loop fusion | bytes 260 | tf_op jit(solution)/shard_map/dynamic_slice | solution.py:286
  95.0 1.3 %dynamic_slice.7 = f32[2,16]{1,0:T(2,128)} dynamic-slice(f32[128,128]{1,0:T(8,128)} %get-tuple-element.5, s32[]{:T(128)S(6)} %select_n.7, s32[]{:T(128)S(6)} %select_n.8), dynamic_slice_sizes={2,16} | dynamic-slice | bytes 260 | tf_op jit(solution)/shard_map/dynamic_slice | solution.py:287
  (1 shorter events, 0.0 us)
Async XLA Ops:
  0.6 4.2 %copy-start = (bf16[64,512]{1,0:T(8,128)(2,1)S(1)}, bf16[64,512]{1,0:T(8,128)(2,1)}, u32[]{:S(2)}) copy-start(bf16[64,512]{1,0:T(8,128)(2,1)} %param.7) | copy-start | bytes 196612
  0.6 5.0 %copy-start.1 = (s32[128]{0:T(128)S(1)}, s32[128]{0:T(128)}, u32[]{:S(2)}) copy-start(s32[128]{0:T(128)} %param.5) | copy-start | bytes 1540

commit v3 on v2

v3 whole, which is shorter than its diff:
```python
import functools

import jax
import jax.numpy as jnp
from jax import lax
from jax.experimental import pallas as pl
from jax.experimental.pallas import tpu as pltpu
from jax.sharding import PartitionSpec as P

BLOCK = 256
PANELS = 2
MESH = pl.DeviceIdType.MESH
ITEMS = (1, 3, 2)
PITCH = 136


def remote(src, dst, send, recv, dev):
    return pltpu.make_async_remote_copy(
        src_ref=src, dst_ref=dst, send_sem=send, recv_sem=recv, device_id=dev, device_id_type=MESH
    )


def await_bytes(ref, sem):
    pltpu.make_async_copy(ref, ref, sem).wait()


def schur_kernel(
    blocks, xt, wt, pos,
    factor_ref, reduced_ref,
    raw, wide, w4, ga, gd, xp, wp, xw, ww, own_q, rbuf, lbuf, acc, part, share, rs, zs,
    loc_sem, x_send, x_recv, w_send, w_recv, z_send, z_recv, v_send, v_recv,
    ya_send, xd_send, ya_recv, xd_recv, cp_sem, sa_send, sd_send, sa_recv, sd_recv, red_send, red_recv,
):
    row = lax.axis_index("row")
    col = lax.axis_index("col")
    zlo, y, x = row // 16, (row // 4) % 4, row % 4
    zhi, core = col // 2, col % 2
    z = zhi * 4 + zlo
    sibling = (row, zhi * 2 + (1 - core))

    def at_z(zz, kk):
        zz = zz % 16
        return ((zz % 4) * 16 + y * 4 + x, (zz // 4) * 2 + kk)

    def at_xy(xx, yy, kk):
        return (zlo * 16 + (yy % 4) * 4 + xx % 4, zhi * 2 + kk)

    def in_plane(m):
        return (x + m % 4) % 4, (y + m // 4) % 4

    barrier = pltpu.get_barrier_semaphore()

    def greet(dev):
        pl.semaphore_signal(barrier, inc=1, device_id=dev, device_id_type=MESH)

    for m in range(1, 16):
        xx, yy = in_plane(m)
        greet(at_xy(xx, yy, core))
        greet(at_xy(xx, yy, 1 - core))
        greet(at_z(z + m, core))
    greet(sibling)

    def cols(h, k=None):
        start = ((h % 4) * 2 + (core if k is None else k)) * 16
        return pl.ds(pl.multiple_of(start, 16), 16)

    half = pl.ds(0, 64)
    loads = [pltpu.make_async_copy(
        blocks.at[:, pl.ds(pl.multiple_of(64 * x, 64), 64)], raw.at[:, half], loc_sem.at[0])]
    for s in range(4):
        loads.append(pltpu.make_async_copy(
            blocks.at[:, pl.ds(pl.multiple_of(64 * s + 16 * y, 16), 16)],
            raw.at[:, pl.ds(64 + 16 * s, 16)], loc_sem.at[1 + s]))
    for load in loads:
        load.start()
    rows = lax.broadcasted_iota(jnp.int32, (128, 128), 0)
    lanes = lax.broadcasted_iota(jnp.int32, (128, 128), 1)
    source = lax.broadcasted_iota(jnp.int32, (512, 128), 0)
    target = lax.broadcasted_iota(jnp.int32, (512, 128), 1)
    place = target // 64 * 256 + target // 16 % 4 * 64 + target % 16
    for yy in range(4):
        order = jnp.where(source == place + 16 * yy, 1.0, 0.0).astype(jnp.bfloat16)
        w4[yy] = jnp.dot(wt[...], order, preferred_element_type=jnp.float32).astype(jnp.bfloat16)
    entry = jnp.broadcast_to(pos[...].astype(jnp.float32), (128, 128))
    own_q[...] = jnp.where(entry.T == (2 * col + lanes // 64).astype(jnp.float32), 1.0, 0.0)
    for load in loads:
        load.wait()

    @pl.loop(0, 16)
    def _(j):
        start = pl.multiple_of(j * PITCH, 8)
        for side in range(2):
            wide[side, pl.ds(start, 128)] = raw[j, :, 128 * side : 128 * side + 128].astype(jnp.float32)

    def one_row(r):
        return jnp.concatenate(
            [wide[side, pl.ds(r, 16, stride=PITCH)] for side in range(2)], axis=1
        ).astype(jnp.bfloat16)

    @pl.loop(0, 64, step=8)
    def _(r):
        for s in range(8):
            ga[r + s, cols(zhi)] = one_row(r + s)
            gd[r + s, cols(zhi)] = one_row(64 + r + s)

    pl.semaphore_wait(barrier, 46)

    quarter = 4 * zlo

    def share_rows(t, h):
        return (
            ga.at[pl.ds(16 * y + t, 4), cols(h)],
            gd.at[pl.ds(16 * x + t, 4), cols(h)],
        )

    own_part = share_rows(quarter, zhi)[0]
    for item in ITEMS:
        remote(own_part, own_part, z_send.at[item], z_recv.at[item], at_z(z + 4 * item, core)).start()

    for m in range(1, 4):
        remote(xt, xp.at[y], x_send, x_recv, at_xy(x, y + m, core)).start()
    for m in range(1, 16):
        xx, yy = in_plane(m)
        remote(w4.at[yy], wp.at[y * 4 + x], w_send, w_recv, at_xy(xx, yy, core)).start()
    pltpu.make_async_copy(xt, xp.at[y], loc_sem.at[0]).start()
    pltpu.make_async_copy(w4.at[y], wp.at[y * 4 + x], loc_sem.at[1]).start()

    own_a, own_d = ga.at[:, cols(zhi)], gd.at[:, cols(zhi)]
    remote(own_a, own_a, sa_send.at[0], sa_recv.at[0], sibling).start()
    remote(own_d, own_d, sd_send.at[0], sd_recv.at[0], sibling).start()

    def multiply(h, k):
        keep = jnp.concatenate([own_q[cols(h, k)]] * 4, axis=1) > 0.5

        @pl.loop(0, 64, step=32)
        def _(d):
            g = gd[pl.ds(d, 32), cols(h, k)].reshape(512, BLOCK)
            full = lax.dot_general(
                g, xw[...], (((1,), (1,)), ((), ())), preferred_element_type=jnp.float32
            ).reshape(32, 16, 512)
            rbuf[pl.ds(d, 32), cols(h, k)] = jnp.where(keep[None], full, 0.0).astype(jnp.bfloat16)

    def spread(t, item):
        a_part, d_part = share_rows(t, zhi + 4 - item)
        for m in range(1, 4):
            remote(a_part, a_part, ya_send.at[item], ya_recv.at[item], at_xy(x, y + m, core)).start()
            remote(a_part, d_part, xd_send.at[item], xd_recv.at[item], at_xy(x + m, y, core)).start()
        pltpu.make_async_copy(a_part, d_part, cp_sem.at[item]).start()

    def hand_over(item):
        await_bytes(ga.at[pl.ds(0, 48), pl.ds(0, 16)], ya_recv.at[item])
        part_a = ga.at[:, cols(zhi + 4 - item)]
        remote(part_a, part_a, sa_send.at[item], sa_recv.at[item], sibling).start()
        await_bytes(ga.at[pl.ds(0, 48), pl.ds(0, 16)], xd_recv.at[item])
        await_bytes(ga.at[pl.ds(0, 16), pl.ds(0, 16)], cp_sem.at[item])
        part_d = gd.at[:, cols(zhi + 4 - item)]
        remote(part_d, part_d, sd_send.at[item], sd_recv.at[item], sibling).start()

    for item in ITEMS:
        a_part, _ = share_rows(quarter, zhi + 4 - item)
        if item == ITEMS[0]:
            pltpu.make_async_copy(xt, xp.at[y], loc_sem.at[0]).wait()
            pltpu.make_async_copy(w4.at[y], wp.at[y * 4 + x], loc_sem.at[1]).wait()
            await_bytes(xp.at[pl.ds(0, 3)], x_recv)
            for p in range(4):
                for q in range(2):
                    xw[128 * p + 64 * q : 128 * p + 64 * q + 64] = xp[p, :, BLOCK * q : BLOCK * q + BLOCK]
            multiply(zhi, core)
        await_bytes(a_part, z_recv.at[item])
        for m in range(1, 4):
            plane = zhi * 4 + (zlo + m) % 4
            remote(a_part, a_part, v_send.at[item], v_recv.at[item, m], at_z(plane, core)).start()
        spread(quarter, item)
    await_bytes(own_a, sa_recv.at[0])
    await_bytes(own_d, sd_recv.at[0])
    multiply(zhi, 1 - core)
    await_bytes(wp.at[pl.ds(0, 15)], w_recv)
    for p in range(4):
        ww[128 * p : 128 * p + 128] = (
            wp[4 * p : 4 * p + 4].reshape(BLOCK, 128).astype(jnp.float32).T.astype(jnp.bfloat16)
        )
    for item in ITEMS:
        for m in range(1, 4):
            t = 4 * ((zlo + 4 - m) % 4)
            await_bytes(share_rows(t, zhi)[0], v_recv.at[item, m])
            spread(t, item)
    for item in ITEMS:
        hand_over(item)
        multiply(zhi + 4 - item, core)
    for item in ITEMS:
        await_bytes(own_a, sa_recv.at[item])
        await_bytes(own_d, sd_recv.at[item])
        multiply(zhi + 4 - item, 1 - core)

    at_p = [pos[...] == 4 * zlo + p for p in range(4)]

    def pick(values, lane):
        total = None
        for p in range(4):
            term = jnp.where(at_p[p], values[128 * p : 128 * p + 128, lane : lane + 128], 0.0)
            total = term if total is None else total + term
        return total

    @pl.loop(0, 64, step=2)
    def _(a):
        g = ga[pl.ds(a, 2)].reshape(256, BLOCK)
        full = lax.dot_general(
            ww[...], g, (((1,), (1,)), ((), ())), preferred_element_type=jnp.float32
        )
        for s in range(2):
            lbuf[pl.ds(pl.multiple_of((a + s) * PITCH, 8), 128)] = pick(full, 128 * s)

    acc[...] = jnp.zeros_like(acc)

    @pl.loop(0, 64, step=4)
    def _(d):
        right = jnp.concatenate(
            [lbuf[pl.ds(q * 64 + d + s, 64, stride=PITCH)].astype(jnp.bfloat16)
             for s in range(4) for q in range(2)], axis=0)
        tiles = [rbuf[d + s] for s in range(4)]
        left = jnp.concatenate(
            [jnp.concatenate([t[:, 128 * p : 128 * p + 128] for t in tiles], axis=1) for p in range(4)],
            axis=0)
        acc[...] += jnp.dot(left, right, preferred_element_type=jnp.float32)

    part[...] = pick(acc[...], 0).T

    me = y * 4 + x
    mine = pl.ds(pl.multiple_of(8 * me, 8), 8)
    for m in range(16):
        xx, yy = in_plane(m)
        theirs = part.at[pl.ds(8 * (yy * 4 + xx), 8)]
        if m:
            remote(theirs, rs.at[core * 16 + me], red_send.at[0], red_recv.at[0], at_xy(xx, yy, core)).start()
        remote(theirs, rs.at[core * 16 + me], red_send.at[0], red_recv.at[0], at_xy(xx, yy, 1 - core)).start()
    rs[core * 16 + me] = part[mine]
    await_bytes(rs.at[pl.ds(0, 31)], red_recv.at[0])
    share[...] = jnp.sum(rs[...], axis=0)
    for m in range(1, 16):
        remote(share, zs.at[z], red_send.at[1], red_recv.at[1], at_z(z + m, core)).start()
    zs[z] = share[...]
    await_bytes(zs.at[pl.ds(0, 15)], red_recv.at[1])
    await_bytes(rs.at[pl.ds(0, 31)], red_send.at[0])
    await_bytes(zs.at[pl.ds(0, 15)], red_send.at[1])
    share[...] = jnp.sum(zs[...], axis=0)
    whole = acc.at[pl.ds(0, 128)]
    for m in range(1, 16):
        xx, yy = in_plane(m)
        remote(share, whole.at[mine], red_send.at[2], red_recv.at[2], at_xy(xx, yy, core)).start()
    whole[mine] = share[...]
    await_bytes(zs.at[pl.ds(0, 15)], red_recv.at[2])
    await_bytes(zs.at[pl.ds(0, 15)], red_send.at[2])

    schur = whole[...]
    factor = jnp.zeros((128, 128), jnp.float32)
    width = 8
    for k in range(PANELS * width):
        lo = k // width * width
        if k == lo:
            inside = (rows >= lo) & (rows < lo + width) & (lanes >= lo) & (lanes < lo + width)
            schur = jnp.where(inside, 0.5 * (schur + schur.T), schur)
        column = jnp.sum(jnp.where(lanes == k, schur, 0.0), axis=1, keepdims=True)
        pivot = jnp.sum(jnp.where(rows[:, :1] == k, column, 0.0), axis=0, keepdims=True)
        column = jnp.where(rows[:, :1] >= k, column / jnp.sqrt(pivot), 0.0)
        line = jnp.sum(jnp.where(rows == lanes, column, 0.0), axis=0, keepdims=True)
        schur = schur - column * line
        factor = jnp.where(lanes == k, column, factor)
    bound = PANELS * width
    part[...] = factor
    near = pl.ds(pl.multiple_of(row // 4 * 8, 8), 8)
    up = (8 - 2 * (row % 4)) % 8
    factor_ref[...] = pltpu.roll(part[near], up, 0)[:2, :bound]
    part[...] = jnp.where((rows >= bound) & (lanes >= bound), schur, 0.0)
    shifted = pltpu.roll(pltpu.roll(part[near], up, 0), (128 - 16 * col) % 128, 1)
    reduced_ref[...] = shifted[:2, :16]

    await_bytes(xp.at[pl.ds(0, 3)], x_send)
    await_bytes(wp.at[pl.ds(0, 15)], w_send)
    for item in ITEMS:
        await_bytes(ga.at[pl.ds(0, 4), pl.ds(0, 16)], z_send.at[item])
        await_bytes(ga.at[pl.ds(0, 12), pl.ds(0, 16)], v_send.at[item])
        await_bytes(ga.at[pl.ds(0, 48), pl.ds(0, 16)], ya_send.at[item])
        await_bytes(ga.at[pl.ds(0, 48), pl.ds(0, 16)], xd_send.at[item])
    for item in range(4):
        await_bytes(ga.at[:, pl.ds(0, 16)], sa_send.at[item])
        await_bytes(gd.at[:, pl.ds(0, 16)], sd_send.at[item])


def on_device(blocks, position, primal, dual_inverse):
    tile_cols = blocks.shape[0]
    rows, width = primal.shape
    per_row = tile_cols * lax.axis_size("col") // lax.axis_size("row")
    count = position.shape[0]
    vmem = pl.BlockSpec(memory_space=pltpu.VMEM)
    hbm = pl.BlockSpec(memory_space=pl.ANY)
    bf, f32 = jnp.bfloat16, jnp.float32
    dma = pltpu.SemaphoreType.DMA
    return pl.pallas_call(
        schur_kernel,
        out_shape=(
            jax.ShapeDtypeStruct((per_row, PANELS * 8), f32),
            jax.ShapeDtypeStruct((per_row, tile_cols), f32),
        ),
        in_specs=[hbm, vmem, vmem, vmem],
        out_specs=(vmem, vmem),
        scratch_shapes=[
            pltpu.VMEM((tile_cols, 128, BLOCK), bf),
            pltpu.VMEM((2, tile_cols * PITCH, 128), f32),
            pltpu.VMEM((4, rows, 128), bf),
            pltpu.VMEM((64, count, BLOCK), bf),
            pltpu.VMEM((64, count, BLOCK), bf),
            pltpu.VMEM((4, rows, width), bf),
            pltpu.VMEM((16, rows, 128), bf),
            pltpu.VMEM((512, BLOCK), bf),
            pltpu.VMEM((512, BLOCK), bf),
            pltpu.VMEM((count, 128), f32),
            pltpu.VMEM((64, count, 512), bf),
            pltpu.VMEM((64 * PITCH, 128), f32),
            pltpu.VMEM((512, count), f32),
            pltpu.VMEM((count, count), f32),
            pltpu.VMEM((8, count), f32),
            pltpu.VMEM((32, 8, count), f32),
            pltpu.VMEM((16, 8, count), f32),
            dma((5,)), dma, dma, dma, dma,
            dma((4,)), dma((4,)), dma((4,)), dma((4, 4)),
            dma((4,)), dma((4,)), dma((4,)), dma((4,)), dma((4,)),
            dma((4,)), dma((4,)), dma((4,)), dma((4,)), dma((3,)), dma((3,)),
        ],
        compiler_params=pltpu.CompilerParams(
            collective_id=0, has_side_effects=True, vmem_limit_bytes=56 << 20
        ),
        name="schur",
    )(blocks, primal, dual_inverse, position.reshape(1, count))


def solution(mesh):
    in_specs = (P("col", None, None), P(), P("row", "col"), P("row", "col"))
    out_specs = (P("row", None), P("row", "col"))
    return jax.shard_map(
        on_device, mesh=mesh, in_specs=in_specs, out_specs=out_specs, check_vma=False
    )
```

time: 97 us -> 86.5 us (0.89)
  local copies, waits for them, and re-layouts: 8.28 us -> 2.44 us
  Pallas kernels: 87.3 us -> 83.1 us
    pallas_call x1, Pallas kernels: 87.3 us -> 83.1 us  [on_device(): pl.pallas_call(schur_kernel, out_shape=(jax.ShapeDtypeStruct((per_row, PA...]
    dynamic_slice x2 -> x0, local copies, waits for them, and re-layouts: 2.55 us -> none  [the longest x1 1.3 us: on_device(): lax.dynamic_slice(schur, (row_id * per_row, col_id * tile_cols), (per_row...]
    unnamed x6 -> x2, local copies, waits for them, and re-layouts: 4.26 us -> 2.44 us
    reshape x2 -> x0, local copies, waits for them, and re-layouts: 1.46 us -> none  [the longest x1 0.73 us: on_device(): position.reshape(count, 1)]
where the time goes in v3:
time: 86.5 us; the launch traced here: 86.1 us
  Pallas kernels  83.1 us (96%)
  local copies, waits for them, and re-layouts  2.44 us (3%)
    pallas_call x1, Pallas kernels, on_device(): pl.pallas_call(schur_kernel, out_shape=(jax.ShapeDtypeStruct((per_row, PA...  83.1 us
    unnamed x2, local copies, waits for them, and re-layouts  2.44 us

profile of v3, /device:TPU:1, one launch (start us, length us, event | category | flops | bytes accessed | tf_op | source)
XLA Modules:
  0.0 86.1 jit_solution(8707377793015659100)
XLA Ops:
  0.6 83.1 %schur.1 = (f32[2,16]{1,0:T(2,128)}, f32[2,16]{1,0:T(2,128)}) custom-call(bf16[16,256,256]{2,1,0:T(8,128)(2,1)} %blocks.1, bf16[64,512]{1,0:T(8,128)(2,1)} %xt.1, bf16[64,512]{1,0:T(8,128)(2,1)} %wt.1, s32[1,128]{1,0:T(1,128)} %bitcast.1), custom_call_target="tpu_custom_call" | custom-call | tf_op jit(solution)/shard_map/schur/pallas_call | solution.py:298
  83.7 1.2 %copy.8 = f32[2,16]{1,0:T(2,128)} copy(f32[2,16]{1,0:T(2,128)} %get-tuple-element.4) | data formatting | bytes 256
  84.9 1.2 %copy.9 = f32[2,16]{1,0:T(2,128)} copy(f32[2,16]{1,0:T(2,128)} %get-tuple-element.5) | data formatting | bytes 256

commit v4 on v3

--- a/solution.py
+++ b/solution.py
@@ -28,8 +28,8 @@
     blocks, xt, wt, pos,
     factor_ref, reduced_ref,
     raw, wide, w4, ga, gd, xp, wp, xw, ww, own_q, rbuf, lbuf, acc, part, share, rs, zs,
-    loc_sem, x_send, x_recv, w_send, w_recv, z_send, z_recv, v_send, v_recv,
-    ya_send, xd_send, ya_recv, xd_recv, cp_sem, sa_send, sd_send, sa_recv, sd_recv, red_send, red_recv,
+    loc_sem, x_send, x_recv, w_send, w_recv, near_send, near_recv, pass_send, z_send, z_recv, v_send, v_recv,
+    ya_send, xd_send, ya_recv, xd_recv, yy_recv, xx_recv, cp_sem, sa_send, sd_send, sa_recv, sd_recv, red_send, red_recv,
 ):
     row = lax.axis_index("row")
     col = lax.axis_index("col")
@@ -114,16 +114,32 @@
         )
 
     own_part = share_rows(quarter, zhi)[0]
-    for item in ITEMS:
-        remote(own_part, own_part, z_send.at[item], z_recv.at[item], at_z(z + 4 * item, core)).start()
-
+
+    remote(own_part, own_part, z_send, z_recv, at_z(z + 8, core)).start()
+
+    def near(way, item, planes):
+        for t in range(0, 16, 4):
+            piece = share_rows(t, zhi)[0]
+            for v in planes:
+                remote(piece, piece, near_send.at[way], near_recv.at[item, t // 4],
+                       at_z(4 * (zhi + item) + v, core)).start()
+
+    @pl.when(zlo == 3)
+    def _():
+        near(0, 1, (0, 2))
+
+    @pl.when(zlo == 0)
+    def _():
+        near(1, 3, (3, 1))
+
+
+    for way, step in ((0, 1), (1, 3)):
+        remote(xt, xp.at[y], x_send, x_recv.at[way], at_xy(x, y + step, core)).start()
     for m in range(1, 4):
-        remote(xt, xp.at[y], x_send, x_recv, at_xy(x, y + m, core)).start()
-    for m in range(1, 16):
-        xx, yy = in_plane(m)
-        remote(w4.at[yy], wp.at[y * 4 + x], w_send, w_recv, at_xy(xx, yy, core)).start()
+        yy = (y + m) % 4
+        remote(w4.at[yy], wp.at[x, y], w_send.at[0], w_recv.at[0], at_xy(x, yy, core)).start()
     pltpu.make_async_copy(xt, xp.at[y], loc_sem.at[0]).start()
-    pltpu.make_async_copy(w4.at[y], wp.at[y * 4 + x], loc_sem.at[1]).start()
+    pltpu.make_async_copy(w4.at[y], wp.at[x, y], loc_sem.at[1]).start()
 
     own_a, own_d = ga.at[:, cols(zhi)], gd.at[:, cols(zhi)]
     remote(own_a, own_a, sa_send.at[0], sa_recv.at[0], sibling).start()
@@ -142,52 +158,106 @@
 
     def spread(t, item):
         a_part, d_part = share_rows(t, zhi + 4 - item)
-        for m in range(1, 4):
-            remote(a_part, a_part, ya_send.at[item], ya_recv.at[item], at_xy(x, y + m, core)).start()
-            remote(a_part, d_part, xd_send.at[item], xd_recv.at[item], at_xy(x + m, y, core)).start()
+        part_half = t // 8
+        for way, step in ((0, 1), (1, 3)):
+            remote(a_part, a_part, ya_send.at[item], ya_recv.at[item, way, part_half],
+                   at_xy(x, y + step, core)).start()
+            remote(a_part, d_part, xd_send.at[item], xd_recv.at[item, way, part_half],
+                   at_xy(x + step, y, core)).start()
         pltpu.make_async_copy(a_part, d_part, cp_sem.at[item]).start()
 
+    eight = ga.at[pl.ds(0, 8), pl.ds(0, 16)]
+
+    def pass_on(item):
+        for way, step in ((0, 1), (1, 3)):
+            back = 4 - step
+            a_part = ga.at[pl.ds((y + back) % 4 * 16 + 8 * way, 8), cols(zhi + 4 - item)]
+            await_bytes(eight, ya_recv.at[item, way, way])
+            remote(a_part, a_part, ya_send.at[item], yy_recv.at[item], at_xy(x, y + step, core)).start()
+            d_part = gd.at[pl.ds((x + back) % 4 * 16 + 8 * way, 8), cols(zhi + 4 - item)]
+            await_bytes(eight, xd_recv.at[item, way, way])
+            remote(d_part, d_part, xd_send.at[item], xx_recv.at[item], at_xy(x + step, y, core)).start()
+
     def hand_over(item):
-        await_bytes(ga.at[pl.ds(0, 48), pl.ds(0, 16)], ya_recv.at[item])
+        for way in range(2):
+            await_bytes(eight, ya_recv.at[item, way, 1 - way])
+        await_bytes(ga.at[pl.ds(0, 16), pl.ds(0, 16)], yy_recv.at[item])
         part_a = ga.at[:, cols(zhi + 4 - item)]
         remote(part_a, part_a, sa_send.at[item], sa_recv.at[item], sibling).start()
-        await_bytes(ga.at[pl.ds(0, 48), pl.ds(0, 16)], xd_recv.at[item])
+        for way in range(2):
+            await_bytes(eight, xd_recv.at[item, way, 1 - way])
+        await_bytes(ga.at[pl.ds(0, 16), pl.ds(0, 16)], xx_recv.at[item])
         await_bytes(ga.at[pl.ds(0, 16), pl.ds(0, 16)], cp_sem.at[item])
         part_d = gd.at[:, cols(zhi + 4 - item)]
         remote(part_d, part_d, sd_send.at[item], sd_recv.at[item], sibling).start()
 
-    for item in ITEMS:
-        a_part, _ = share_rows(quarter, zhi + 4 - item)
-        if item == ITEMS[0]:
-            pltpu.make_async_copy(xt, xp.at[y], loc_sem.at[0]).wait()
-            pltpu.make_async_copy(w4.at[y], wp.at[y * 4 + x], loc_sem.at[1]).wait()
-            await_bytes(xp.at[pl.ds(0, 3)], x_recv)
-            for p in range(4):
-                for q in range(2):
-                    xw[128 * p + 64 * q : 128 * p + 64 * q + 64] = xp[p, :, BLOCK * q : BLOCK * q + BLOCK]
-            multiply(zhi, core)
-        await_bytes(a_part, z_recv.at[item])
+    odd = zlo % 2
+    early, late = 1 + 2 * odd, 3 - 2 * odd
+    onward = at_z(z + 17 - 2 * odd, core)
+
+    def from_early(t):
+        await_bytes(own_part, near_recv.at[early, t // 4])
+        piece = share_rows(t, zhi + 4 - early)[0]
+        remote(piece, piece, pass_send, near_recv.at[early, t // 4], onward).start()
+        spread(t, early)
+
+    def from_late(t):
+        await_bytes(own_part, near_recv.at[late, t // 4])
+        spread(t, late)
+
+    def from_far():
+        a_part, _ = share_rows(quarter, zhi + 2)
+        await_bytes(a_part, z_recv)
         for m in range(1, 4):
             plane = zhi * 4 + (zlo + m) % 4
-            remote(a_part, a_part, v_send.at[item], v_recv.at[item, m], at_z(plane, core)).start()
-        spread(quarter, item)
+            remote(a_part, a_part, v_send, v_recv.at[m], at_z(plane, core)).start()
+        spread(quarter, 2)
+
+    def from_planes():
+        for m in range(1, 4):
+            t = 4 * ((zlo + 4 - m) % 4)
+            await_bytes(own_part, v_recv.at[m])
+            spread(t, 2)
+
+    for way, step in ((0, 1), (1, 3)):
+        x_part = xp.at[(y + 4 - step) % 4, pl.ds(32 * way, 32)]
+        await_bytes(xp.at[0], x_recv.at[way])
+        remote(x_part, x_part, x_send, x_recv.at[2], at_xy(x, y + step, core)).start()
+    pltpu.make_async_copy(w4.at[y], wp.at[x, y], loc_sem.at[1]).wait()
+    await_bytes(wp.at[0, pl.ds(0, 3)], w_recv.at[0])
+    for m in range(1, 4):
+        remote(wp.at[x], wp.at[x], w_send.at[1], w_recv.at[1], at_xy(x + m, y, core)).start()
+    from_early(0)
+    pltpu.make_async_copy(xt, xp.at[y], loc_sem.at[0]).wait()
+    await_bytes(xp.at[0], x_recv.at[2])
+    for p in range(4):
+        for q in range(2):
+            xw[128 * p + 64 * q : 128 * p + 64 * q + 64] = xp[p, :, BLOCK * q : BLOCK * q + BLOCK]
+    multiply(zhi, core)
+    from_early(4)
+    from_late(0)
+    from_far()
+    from_early(8)
+    from_late(4)
+    from_early(12)
+    from_late(8)
+    from_late(12)
+    from_planes()
+    pass_on(early)
+    pass_on(late)
+    pass_on(2)
     await_bytes(own_a, sa_recv.at[0])
     await_bytes(own_d, sd_recv.at[0])
     multiply(zhi, 1 - core)
-    await_bytes(wp.at[pl.ds(0, 15)], w_recv)
+    await_bytes(wp.at[pl.ds(0, 3)], w_recv.at[1])
     for p in range(4):
         ww[128 * p : 128 * p + 128] = (
-            wp[4 * p : 4 * p + 4].reshape(BLOCK, 128).astype(jnp.float32).T.astype(jnp.bfloat16)
+            wp[:, p].reshape(BLOCK, 128).astype(jnp.float32).T.astype(jnp.bfloat16)
         )
-    for item in ITEMS:
-        for m in range(1, 4):
-            t = 4 * ((zlo + 4 - m) % 4)
-            await_bytes(share_rows(t, zhi)[0], v_recv.at[item, m])
-            spread(t, item)
-    for item in ITEMS:
+    for item in (early, late, 2):
         hand_over(item)
         multiply(zhi + 4 - item, core)
-    for item in ITEMS:
+    for item in (early, late, 2):
         await_bytes(own_a, sa_recv.at[item])
         await_bytes(own_d, sd_recv.at[item])
         multiply(zhi + 4 - item, 1 - core)
@@ -201,13 +271,13 @@
             total = term if total is None else total + term
         return total
 
-    @pl.loop(0, 64, step=2)
+    @pl.loop(0, 64, step=4)
     def _(a):
-        g = ga[pl.ds(a, 2)].reshape(256, BLOCK)
+        g = ga[pl.ds(a, 4)].reshape(512, BLOCK)
         full = lax.dot_general(
             ww[...], g, (((1,), (1,)), ((), ())), preferred_element_type=jnp.float32
         )
-        for s in range(2):
+        for s in range(4):
             lbuf[pl.ds(pl.multiple_of((a + s) * PITCH, 8), 128)] = pick(full, 128 * s)
 
     acc[...] = jnp.zeros_like(acc)
@@ -275,12 +345,23 @@
     reduced_ref[...] = shifted[:2, :16]
 
     await_bytes(xp.at[pl.ds(0, 3)], x_send)
-    await_bytes(wp.at[pl.ds(0, 15)], w_send)
+    await_bytes(wp.at[0, pl.ds(0, 3)], w_send.at[0])
+    await_bytes(wp.at[pl.ds(0, 3)], w_send.at[1])
     for item in ITEMS:
-        await_bytes(ga.at[pl.ds(0, 4), pl.ds(0, 16)], z_send.at[item])
-        await_bytes(ga.at[pl.ds(0, 12), pl.ds(0, 16)], v_send.at[item])
         await_bytes(ga.at[pl.ds(0, 48), pl.ds(0, 16)], ya_send.at[item])
         await_bytes(ga.at[pl.ds(0, 48), pl.ds(0, 16)], xd_send.at[item])
+    await_bytes(own_part, z_send)
+    await_bytes(ga.at[pl.ds(0, 16), pl.ds(0, 16)], pass_send)
+    await_bytes(ga.at[pl.ds(0, 12), pl.ds(0, 16)], v_send)
+
+    @pl.when(zlo == 3)
+    def _():
+        await_bytes(ga.at[pl.ds(0, 32), pl.ds(0, 16)], near_send.at[0])
+
+    @pl.when(zlo == 0)
+    def _():
+        await_bytes(ga.at[pl.ds(0, 32), pl.ds(0, 16)], near_send.at[1])
+
     for item in range(4):
         await_bytes(ga.at[:, pl.ds(0, 16)], sa_send.at[item])
         await_bytes(gd.at[:, pl.ds(0, 16)], sd_send.at[item])
@@ -310,7 +391,7 @@
             pltpu.VMEM((64, count, BLOCK), bf),
             pltpu.VMEM((64, count, BLOCK), bf),
             pltpu.VMEM((4, rows, width), bf),
-            pltpu.VMEM((16, rows, 128), bf),
+            pltpu.VMEM((4, 4, rows, 128), bf),
             pltpu.VMEM((512, BLOCK), bf),
             pltpu.VMEM((512, BLOCK), bf),
             pltpu.VMEM((count, 128), f32),
@@ -321,9 +402,9 @@
             pltpu.VMEM((8, count), f32),
             pltpu.VMEM((32, 8, count), f32),
             pltpu.VMEM((16, 8, count), f32),
-            dma((5,)), dma, dma, dma, dma,
-            dma((4,)), dma((4,)), dma((4,)), dma((4, 4)),
-            dma((4,)), dma((4,)), dma((4,)), dma((4,)), dma((4,)),
+            dma((5,)), dma, dma((3,)), dma((2,)), dma((2,)),
+            dma((2,)), dma((4, 4)), dma, dma, dma, dma, dma((4,)),
+            dma((4,)), dma((4,)), dma((4, 2, 2)), dma((4, 2, 2)), dma((4,)), dma((4,)), dma((4,)),
             dma((4,)), dma((4,)), dma((4,)), dma((4,)), dma((3,)), dma((3,)),
         ],
         compiler_params=pltpu.CompilerParams(

time: 86.5 us -> 78.5 us (0.908)
  Pallas kernels: 83.1 us -> 75.2 us
    pallas_call x1, Pallas kernels: 83.1 us -> 75.2 us  [on_device(): pl.pallas_call(schur_kernel, out_shape=(jax.ShapeDtypeStruct((per_row, PA...]
where the time goes in v4:
time: 78.5 us; the launch traced here: 78.2 us
  Pallas kernels  75.2 us (96%)
  local copies, waits for them, and re-layouts  2.44 us (3%)
    pallas_call x1, Pallas kernels, on_device(): pl.pallas_call(schur_kernel, out_shape=(jax.ShapeDtypeStruct((per_row, PA...  75.2 us
    unnamed x2, local copies, waits for them, and re-layouts  2.44 us

profile of v4, /device:TPU:1, one launch (start us, length us, event | category | flops | bytes accessed | tf_op | source)
XLA Modules:
  0.0 78.2 jit_solution(17219127691072624859)
XLA Ops:
  0.6 75.2 %schur.1 = (f32[2,16]{1,0:T(2,128)}, f32[2,16]{1,0:T(2,128)}) custom-call(bf16[16,256,256]{2,1,0:T(8,128)(2,1)} %blocks.1, bf16[64,512]{1,0:T(8,128)(2,1)} %xt.1, bf16[64,512]{1,0:T(8,128)(2,1)} %wt.1, s32[1,128]{1,0:T(1,128)} %bitcast.1), custom_call_target="tpu_custom_call" | custom-call | tf_op jit(solution)/shard_map/schur/pallas_call | solution.py:379
  75.8 1.2 %copy.8 = f32[2,16]{1,0:T(2,128)} copy(f32[2,16]{1,0:T(2,128)} %get-tuple-element.4) | data formatting | bytes 256
  77.0 1.2 %copy.9 = f32[2,16]{1,0:T(2,128)} copy(f32[2,16]{1,0:T(2,128)} %get-tuple-element.5) | data formatting | bytes 256

commit v5 on v4

--- a/solution.py
+++ b/solution.py
@@ -26,8 +26,8 @@
 
 def schur_kernel(
     blocks, xt, wt, pos,
-    factor_ref, reduced_ref,
-    raw, wide, w4, ga, gd, xp, wp, xw, ww, own_q, rbuf, lbuf, acc, part, share, rs, zs,
+    out_ref,
+    raw, wide, w4, ga, gd, xp, wp, xw, ww, own_q, rbuf, lbuf, acc, part, other, both, share, rs, zs,
     loc_sem, x_send, x_recv, w_send, w_recv, near_send, near_recv, pass_send, z_send, z_recv, v_send, v_recv,
     ya_send, xd_send, ya_recv, xd_recv, yy_recv, xx_recv, cp_sem, sa_send, sd_send, sa_recv, sd_recv, red_send, red_recv,
 ):
@@ -56,7 +56,6 @@
     for m in range(1, 16):
         xx, yy = in_plane(m)
         greet(at_xy(xx, yy, core))
-        greet(at_xy(xx, yy, 1 - core))
         greet(at_z(z + m, core))
     greet(sibling)
 
@@ -64,15 +63,67 @@
         start = ((h % 4) * 2 + (core if k is None else k)) * 16
         return pl.ds(pl.multiple_of(start, 16), 16)
 
-    half = pl.ds(0, 64)
+    first = pltpu.make_async_copy(
+        blocks.at[:, pl.ds(pl.multiple_of(64 * x + 16 * y, 16), 16)], raw.at[:, pl.ds(128, 16)], loc_sem.at[5])
+    first.start()
     loads = [pltpu.make_async_copy(
-        blocks.at[:, pl.ds(pl.multiple_of(64 * x, 64), 64)], raw.at[:, half], loc_sem.at[0])]
+        blocks.at[:, pl.ds(pl.multiple_of(64 * x, 64), 64)], raw.at[:, pl.ds(0, 64)], loc_sem.at[0])]
     for s in range(4):
         loads.append(pltpu.make_async_copy(
             blocks.at[:, pl.ds(pl.multiple_of(64 * s + 16 * y, 16), 16)],
             raw.at[:, pl.ds(64 + 16 * s, 16)], loc_sem.at[1 + s]))
     for load in loads:
         load.start()
+
+    def one_row(r):
+        return jnp.concatenate(
+            [wide[side, pl.ds(r, 16, stride=PITCH)] for side in range(2)], axis=1
+        ).astype(jnp.bfloat16)
+
+    first.wait()
+    for j in range(16):
+        for side in range(2):
+            wide[side, j * PITCH : j * PITCH + 16] = (
+                raw[j, 128:144, 128 * side : 128 * side + 128].astype(jnp.float32))
+    for r in range(16):
+        line = one_row(r)
+        ga[16 * y + r, cols(zhi)] = line
+        gd[16 * x + r, cols(zhi)] = line
+
+    pl.semaphore_wait(barrier, 31)
+
+    quarter = 4 * zlo
+
+    def share_rows(t, h):
+        return (
+            ga.at[pl.ds(16 * y + t, 4), cols(h)],
+            gd.at[pl.ds(16 * x + t, 4), cols(h)],
+        )
+
+    own_part = share_rows(quarter, zhi)[0]
+
+    remote(own_part, own_part, z_send, z_recv, at_z(z + 8, core)).start()
+
+    def near(way, item, planes):
+        for t in range(0, 16, 4):
+            piece = share_rows(t, zhi)[0]
+            for v in planes:
+                remote(piece, piece, near_send.at[way], near_recv.at[item, t // 4],
+                       at_z(4 * (zhi + item) + v, core)).start()
+
+    @pl.when(zlo == 3)
+    def _():
+        near(0, 1, (0, 2))
+
+    @pl.when(zlo == 0)
+    def _():
+        near(1, 3, (3, 1))
+
+
+    for way, step in ((0, 1), (1, 3)):
+        remote(xt, xp.at[y], x_send, x_recv.at[way], at_xy(x, y + step, core)).start()
+    pltpu.make_async_copy(xt, xp.at[y], loc_sem.at[6]).start()
+
     rows = lax.broadcasted_iota(jnp.int32, (128, 128), 0)
     lanes = lax.broadcasted_iota(jnp.int32, (128, 128), 1)
     source = lax.broadcasted_iota(jnp.int32, (512, 128), 0)
@@ -81,8 +132,10 @@
     for yy in range(4):
         order = jnp.where(source == place + 16 * yy, 1.0, 0.0).astype(jnp.bfloat16)
         w4[yy] = jnp.dot(wt[...], order, preferred_element_type=jnp.float32).astype(jnp.bfloat16)
-    entry = jnp.broadcast_to(pos[...].astype(jnp.float32), (128, 128))
-    own_q[...] = jnp.where(entry.T == (2 * col + lanes // 64).astype(jnp.float32), 1.0, 0.0)
+    for m in range(1, 4):
+        yy = (y + m) % 4
+        remote(w4.at[yy], wp.at[x, y], w_send.at[0], w_recv.at[0], at_xy(x, yy, core)).start()
+    pltpu.make_async_copy(w4.at[y], wp.at[x, y], loc_sem.at[7]).start()
     for load in loads:
         load.wait()
 
@@ -90,59 +143,22 @@
     def _(j):
         start = pl.multiple_of(j * PITCH, 8)
         for side in range(2):
-            wide[side, pl.ds(start, 128)] = raw[j, :, 128 * side : 128 * side + 128].astype(jnp.float32)
-
-    def one_row(r):
-        return jnp.concatenate(
-            [wide[side, pl.ds(r, 16, stride=PITCH)] for side in range(2)], axis=1
-        ).astype(jnp.bfloat16)
-
-    @pl.loop(0, 64, step=8)
-    def _(r):
-        for s in range(8):
-            ga[r + s, cols(zhi)] = one_row(r + s)
-            gd[r + s, cols(zhi)] = one_row(64 + r + s)
-
-    pl.semaphore_wait(barrier, 46)
-
-    quarter = 4 * zlo
-
-    def share_rows(t, h):
-        return (
-            ga.at[pl.ds(16 * y + t, 4), cols(h)],
-            gd.at[pl.ds(16 * x + t, 4), cols(h)],
-        )
-
-    own_part = share_rows(quarter, zhi)[0]
-
-    remote(own_part, own_part, z_send, z_recv, at_z(z + 8, core)).start()
-
-    def near(way, item, planes):
-        for t in range(0, 16, 4):
-            piece = share_rows(t, zhi)[0]
-            for v in planes:
-                remote(piece, piece, near_send.at[way], near_recv.at[item, t // 4],
-                       at_z(4 * (zhi + item) + v, core)).start()
-
-    @pl.when(zlo == 3)
-    def _():
-        near(0, 1, (0, 2))
-
-    @pl.when(zlo == 0)
-    def _():
-        near(1, 3, (3, 1))
-
-
-    for way, step in ((0, 1), (1, 3)):
-        remote(xt, xp.at[y], x_send, x_recv.at[way], at_xy(x, y + step, core)).start()
+            wide[side, pl.ds(start, 128)] = raw[j, 0:128, 128 * side : 128 * side + 128].astype(jnp.float32)
+
     for m in range(1, 4):
-        yy = (y + m) % 4
-        remote(w4.at[yy], wp.at[x, y], w_send.at[0], w_recv.at[0], at_xy(x, yy, core)).start()
-    pltpu.make_async_copy(xt, xp.at[y], loc_sem.at[0]).start()
-    pltpu.make_async_copy(w4.at[y], wp.at[x, y], loc_sem.at[1]).start()
+        a_start, d_start = (y + m) % 4 * 16, (x + m) % 4 * 16
+
+        @pl.loop(0, 16, step=8)
+        def _(r):
+            for s in range(8):
+                ga[a_start + r + s, cols(zhi)] = one_row(a_start + r + s)
+                gd[d_start + r + s, cols(zhi)] = one_row(64 + d_start + r + s)
+
+    entry = jnp.broadcast_to(pos[...].astype(jnp.float32), (128, 128))
+    own_q[...] = jnp.where(entry.T == (2 * col + lanes // 64).astype(jnp.float32), 1.0, 0.0)
 
     own_a, own_d = ga.at[:, cols(zhi)], gd.at[:, cols(zhi)]
-    remote(own_a, own_a, sa_send.at[0], sa_recv.at[0], sibling).start()
+    remote(own_a, own_a, sa_send.at[0, 0], sa_recv.at[0, 0], sibling).start()
     remote(own_d, own_d, sd_send.at[0], sd_recv.at[0], sibling).start()
 
     def multiply(h, k):
@@ -178,18 +194,48 @@
             await_bytes(eight, xd_recv.at[item, way, way])
             remote(d_part, d_part, xd_send.at[item], xx_recv.at[item], at_xy(x + step, y, core)).start()
 
+    sixteen = ga.at[pl.ds(0, 16), pl.ds(0, 16)]
+
+    def hand_rows(item, m):
+        part = ga.at[pl.ds((y + m) % 4 * 16, 16), cols(zhi + 4 - item)]
+        remote(part, part, sa_send.at[item, m], sa_recv.at[item, m], sibling).start()
+
     def hand_over(item):
         for way in range(2):
             await_bytes(eight, ya_recv.at[item, way, 1 - way])
-        await_bytes(ga.at[pl.ds(0, 16), pl.ds(0, 16)], yy_recv.at[item])
-        part_a = ga.at[:, cols(zhi + 4 - item)]
-        remote(part_a, part_a, sa_send.at[item], sa_recv.at[item], sibling).start()
+            hand_rows(item, 3 - 2 * way)
+        await_bytes(sixteen, yy_recv.at[item])
+        hand_rows(item, 2)
         for way in range(2):
             await_bytes(eight, xd_recv.at[item, way, 1 - way])
-        await_bytes(ga.at[pl.ds(0, 16), pl.ds(0, 16)], xx_recv.at[item])
-        await_bytes(ga.at[pl.ds(0, 16), pl.ds(0, 16)], cp_sem.at[item])
+        await_bytes(sixteen, xx_recv.at[item])
+        await_bytes(sixteen, cp_sem.at[item])
         part_d = gd.at[:, cols(zhi + 4 - item)]
         remote(part_d, part_d, sd_send.at[item], sd_recv.at[item], sibling).start()
+
+    at_p = [pos[...] == 4 * zlo + p for p in range(4)]
+
+    def pick(values, lane):
+        total = None
+        for p in range(4):
+            term = jnp.where(at_p[p], values[128 * p : 128 * p + 128, lane : lane + 128], 0.0)
+            total = term if total is None else total + term
+        return total
+
+    def left_rows(m):
+        for item in ITEMS:
+            await_bytes(sixteen, sa_recv.at[item, m])
+        start = (y + m) % 4 * 16
+
+        @pl.loop(0, 16, step=8)
+        def _(r):
+            a = start + r
+            g = ga[pl.ds(a, 8)].reshape(1024, BLOCK)
+            full = lax.dot_general(
+                ww[...], g, (((1,), (1,)), ((), ())), preferred_element_type=jnp.float32
+            )
+            for s in range(8):
+                lbuf[pl.ds(pl.multiple_of((a + s) * PITCH, 8), 128)] = pick(full, 128 * s)
 
     odd = zlo % 2
     early, late = 1 + 2 * odd, 3 - 2 * odd
@@ -223,12 +269,12 @@
         x_part = xp.at[(y + 4 - step) % 4, pl.ds(32 * way, 32)]
         await_bytes(xp.at[0], x_recv.at[way])
         remote(x_part, x_part, x_send, x_recv.at[2], at_xy(x, y + step, core)).start()
-    pltpu.make_async_copy(w4.at[y], wp.at[x, y], loc_sem.at[1]).wait()
+    pltpu.make_async_copy(w4.at[y], wp.at[x, y], loc_sem.at[7]).wait()
     await_bytes(wp.at[0, pl.ds(0, 3)], w_recv.at[0])
     for m in range(1, 4):
         remote(wp.at[x], wp.at[x], w_send.at[1], w_recv.at[1], at_xy(x + m, y, core)).start()
     from_early(0)
-    pltpu.make_async_copy(xt, xp.at[y], loc_sem.at[0]).wait()
+    pltpu.make_async_copy(xt, xp.at[y], loc_sem.at[6]).wait()
     await_bytes(xp.at[0], x_recv.at[2])
     for p in range(4):
         for q in range(2):
@@ -242,11 +288,14 @@
     from_early(12)
     from_late(8)
     from_late(12)
+    hand_rows(early, 0)
+    hand_rows(late, 0)
     from_planes()
+    hand_rows(2, 0)
     pass_on(early)
     pass_on(late)
     pass_on(2)
-    await_bytes(own_a, sa_recv.at[0])
+    await_bytes(own_a, sa_recv.at[0, 0])
     await_bytes(own_d, sd_recv.at[0])
     multiply(zhi, 1 - core)
     await_bytes(wp.at[pl.ds(0, 3)], w_recv.at[1])
@@ -254,40 +303,32 @@
         ww[128 * p : 128 * p + 128] = (
             wp[:, p].reshape(BLOCK, 128).astype(jnp.float32).T.astype(jnp.bfloat16)
         )
-    for item in (early, late, 2):
-        hand_over(item)
-        multiply(zhi + 4 - item, core)
-    for item in (early, late, 2):
-        await_bytes(own_a, sa_recv.at[item])
+    def from_sibling(item):
         await_bytes(own_d, sd_recv.at[item])
         multiply(zhi + 4 - item, 1 - core)
 
-    at_p = [pos[...] == 4 * zlo + p for p in range(4)]
-
-    def pick(values, lane):
-        total = None
-        for p in range(4):
-            term = jnp.where(at_p[p], values[128 * p : 128 * p + 128, lane : lane + 128], 0.0)
-            total = term if total is None else total + term
-        return total
-
-    @pl.loop(0, 64, step=4)
-    def _(a):
-        g = ga[pl.ds(a, 4)].reshape(512, BLOCK)
-        full = lax.dot_general(
-            ww[...], g, (((1,), (1,)), ((), ())), preferred_element_type=jnp.float32
-        )
-        for s in range(4):
-            lbuf[pl.ds(pl.multiple_of((a + s) * PITCH, 8), 128)] = pick(full, 128 * s)
+    hand_over(early)
+    multiply(zhi + 4 - early, core)
+    hand_over(late)
+    multiply(zhi + 4 - late, core)
+    left_rows(0)
+    hand_over(2)
+    multiply(zhi + 2, core)
+    from_sibling(early)
+    left_rows(1)
+    from_sibling(late)
+    left_rows(3)
+    from_sibling(2)
+    left_rows(2)
 
     acc[...] = jnp.zeros_like(acc)
 
-    @pl.loop(0, 64, step=4)
+    @pl.loop(0, 64, step=16)
     def _(d):
         right = jnp.concatenate(
             [lbuf[pl.ds(q * 64 + d + s, 64, stride=PITCH)].astype(jnp.bfloat16)
-             for s in range(4) for q in range(2)], axis=0)
-        tiles = [rbuf[d + s] for s in range(4)]
+             for s in range(16) for q in range(2)], axis=0)
+        tiles = [rbuf[d + s] for s in range(16)]
         left = jnp.concatenate(
             [jnp.concatenate([t[:, 128 * p : 128 * p + 128] for t in tiles], axis=1) for p in range(4)],
             axis=0)
@@ -297,20 +338,22 @@
 
     me = y * 4 + x
     mine = pl.ds(pl.multiple_of(8 * me, 8), 8)
-    for m in range(16):
+    remote(part, other, red_send.at[3], red_recv.at[3], sibling).start()
+    await_bytes(part, red_recv.at[3])
+    both[...] = part[...] + other[...]
+    for m in range(1, 16):
         xx, yy = in_plane(m)
-        theirs = part.at[pl.ds(8 * (yy * 4 + xx), 8)]
-        if m:
-            remote(theirs, rs.at[core * 16 + me], red_send.at[0], red_recv.at[0], at_xy(xx, yy, core)).start()
-        remote(theirs, rs.at[core * 16 + me], red_send.at[0], red_recv.at[0], at_xy(xx, yy, 1 - core)).start()
-    rs[core * 16 + me] = part[mine]
-    await_bytes(rs.at[pl.ds(0, 31)], red_recv.at[0])
+        theirs = both.at[pl.ds(8 * (yy * 4 + xx), 8)]
+        remote(theirs, rs.at[me], red_send.at[0], red_recv.at[0], at_xy(xx, yy, core)).start()
+    rs[me] = both[mine]
+    await_bytes(rs.at[pl.ds(0, 15)], red_recv.at[0])
     share[...] = jnp.sum(rs[...], axis=0)
     for m in range(1, 16):
         remote(share, zs.at[z], red_send.at[1], red_recv.at[1], at_z(z + m, core)).start()
     zs[z] = share[...]
     await_bytes(zs.at[pl.ds(0, 15)], red_recv.at[1])
-    await_bytes(rs.at[pl.ds(0, 31)], red_send.at[0])
+    await_bytes(rs.at[pl.ds(0, 15)], red_send.at[0])
+    await_bytes(part, red_send.at[3])
     await_bytes(zs.at[pl.ds(0, 15)], red_send.at[1])
     share[...] = jnp.sum(zs[...], axis=0)
     whole = acc.at[pl.ds(0, 128)]
@@ -339,10 +382,10 @@
     part[...] = factor
     near = pl.ds(pl.multiple_of(row // 4 * 8, 8), 8)
     up = (8 - 2 * (row % 4)) % 8
-    factor_ref[...] = pltpu.roll(part[near], up, 0)[:2, :bound]
+    top = pltpu.roll(part[near], up, 0)
     part[...] = jnp.where((rows >= bound) & (lanes >= bound), schur, 0.0)
-    shifted = pltpu.roll(pltpu.roll(part[near], up, 0), (128 - 16 * col) % 128, 1)
-    reduced_ref[...] = shifted[:2, :16]
+    shifted = pltpu.roll(pltpu.roll(part[near], up, 0), (128 + bound - 16 * col) % 128, 1)
+    out_ref[...] = jnp.where(lanes[:8] < bound, top, shifted)[:2, : bound + 16]
 
     await_bytes(xp.at[pl.ds(0, 3)], x_send)
     await_bytes(wp.at[0, pl.ds(0, 3)], w_send.at[0])
@@ -363,8 +406,11 @@
         await_bytes(ga.at[pl.ds(0, 32), pl.ds(0, 16)], near_send.at[1])
 
     for item in range(4):
-        await_bytes(ga.at[:, pl.ds(0, 16)], sa_send.at[item])
         await_bytes(gd.at[:, pl.ds(0, 16)], sd_send.at[item])
+    await_bytes(own_a, sa_send.at[0, 0])
+    for item in ITEMS:
+        for m in range(4):
+            await_bytes(sixteen, sa_send.at[item, m])
 
 
 def on_device(blocks, position, primal, dual_inverse):
@@ -376,16 +422,13 @@
     hbm = pl.BlockSpec(memory_space=pl.ANY)
     bf, f32 = jnp.bfloat16, jnp.float32
     dma = pltpu.SemaphoreType.DMA
-    return pl.pallas_call(
+    both = pl.pallas_call(
         schur_kernel,
-        out_shape=(
-            jax.ShapeDtypeStruct((per_row, PANELS * 8), f32),
-            jax.ShapeDtypeStruct((per_row, tile_cols), f32),
-        ),
+        out_shape=jax.ShapeDtypeStruct((per_row, PANELS * 8 + tile_cols), f32),
         in_specs=[hbm, vmem, vmem, vmem],
-        out_specs=(vmem, vmem),
+        out_specs=vmem,
         scratch_shapes=[
-            pltpu.VMEM((tile_cols, 128, BLOCK), bf),
+            pltpu.VMEM((tile_cols, 144, BLOCK), bf),
             pltpu.VMEM((2, tile_cols * PITCH, 128), f32),
             pltpu.VMEM((4, rows, 128), bf),
             pltpu.VMEM((64, count, BLOCK), bf),
@@ -399,19 +442,22 @@
             pltpu.VMEM((64 * PITCH, 128), f32),
             pltpu.VMEM((512, count), f32),
             pltpu.VMEM((count, count), f32),
+            pltpu.VMEM((count, count), f32),
+            pltpu.VMEM((count, count), f32),
             pltpu.VMEM((8, count), f32),
-            pltpu.VMEM((32, 8, count), f32),
             pltpu.VMEM((16, 8, count), f32),
-            dma((5,)), dma, dma((3,)), dma((2,)), dma((2,)),
+            pltpu.VMEM((16, 8, count), f32),
+            dma((8,)), dma, dma((3,)), dma((2,)), dma((2,)),
             dma((2,)), dma((4, 4)), dma, dma, dma, dma, dma((4,)),
             dma((4,)), dma((4,)), dma((4, 2, 2)), dma((4, 2, 2)), dma((4,)), dma((4,)), dma((4,)),
-            dma((4,)), dma((4,)), dma((4,)), dma((4,)), dma((3,)), dma((3,)),
+            dma((4, 4)), dma((4,)), dma((4, 4)), dma((4,)), dma((4,)), dma((4,)),
         ],
         compiler_params=pltpu.CompilerParams(
             collective_id=0, has_side_effects=True, vmem_limit_bytes=56 << 20
         ),
         name="schur",
     )(blocks, primal, dual_inverse, position.reshape(1, count))
+    return both[:, : PANELS * 8], both[:, PANELS * 8 :]
 
 
 def solution(mesh):

time: 78.5 us -> 73.1 us (0.931)
  Pallas kernels: 75.2 us -> 70.9 us
  local copies, waits for them, and re-layouts: 2.44 us -> 1.37 us
    pallas_call x1, Pallas kernels: 75.2 us -> 70.9 us  [on_device(): pl.pallas_call(schur_kernel, out_shape=jax.ShapeDtypeStruct((per_row, PAN...]
    unnamed x2 -> x0, local copies, waits for them, and re-layouts: 2.44 us -> none
    slice x0 -> x1, local copies, waits for them, and re-layouts: none -> 1.37 us  [on_device(): return (both[:, :PANELS * 8], both[:, PANELS * 8:])]
where the time goes in v5:
time: 73.1 us; the launch traced here: 72.9 us
  Pallas kernels  70.9 us (97%)
  local copies, waits for them, and re-layouts  1.37 us (2%)
    pallas_call x1, Pallas kernels, on_device(): pl.pallas_call(schur_kernel, out_shape=jax.ShapeDtypeStruct((per_row, PAN...  70.9 us

profile of v5, /device:TPU:1, one launch (start us, length us, event | category | flops | bytes accessed | tf_op | source)
XLA Modules:
  0.0 72.9 jit_solution(650020888076860014)
XLA Ops:
  0.6 70.9 %schur.1 = f32[2,32]{1,0:T(2,128)} custom-call(bf16[16,256,256]{2,1,0:T(8,128)(2,1)} %blocks.1, bf16[64,512]{1,0:T(8,128)(2,1)} %xt.1, bf16[64,512]{1,0:T(8,128)(2,1)} %wt.1, s32[1,128]{1,0:T(1,128)} %bitcast.1), custom_call_target="tpu_custom_call" | custom-call | tf_op jit(solution)/shard_map/schur/pallas_call | solution.py:425
  71.5 1.4 %fusion = (f32[2,16]{1,0:T(2,128)}, f32[2,16]{1,0:T(2,128)}) fusion(f32[2,32]{1,0:T(2,128)} %schur.1), kind=kLoop, calls=%fused_computation | loop fusion | bytes 512 | tf_op jit(solution)/shard_map/slice | solution.py:460

commit v6 on v5

--- a/solution.py
+++ b/solution.py
@@ -164,13 +164,13 @@
     def multiply(h, k):
         keep = jnp.concatenate([own_q[cols(h, k)]] * 4, axis=1) > 0.5
 
-        @pl.loop(0, 64, step=32)
+        @pl.loop(0, 64, step=64)
         def _(d):
-            g = gd[pl.ds(d, 32), cols(h, k)].reshape(512, BLOCK)
+            g = gd[pl.ds(d, 64), cols(h, k)].reshape(1024, BLOCK)
             full = lax.dot_general(
                 g, xw[...], (((1,), (1,)), ((), ())), preferred_element_type=jnp.float32
-            ).reshape(32, 16, 512)
-            rbuf[pl.ds(d, 32), cols(h, k)] = jnp.where(keep[None], full, 0.0).astype(jnp.bfloat16)
+            ).reshape(64, 16, 512)
+            rbuf[pl.ds(d, 64), cols(h, k)] = jnp.where(keep[None], full, 0.0).astype(jnp.bfloat16)
 
     def spread(t, item):
         a_part, d_part = share_rows(t, zhi + 4 - item)
@@ -227,14 +227,14 @@
             await_bytes(sixteen, sa_recv.at[item, m])
         start = (y + m) % 4 * 16
 
-        @pl.loop(0, 16, step=8)
+        @pl.loop(0, 16, step=16)
         def _(r):
             a = start + r
-            g = ga[pl.ds(a, 8)].reshape(1024, BLOCK)
+            g = ga[pl.ds(a, 16)].reshape(2048, BLOCK)
             full = lax.dot_general(
                 ww[...], g, (((1,), (1,)), ((), ())), preferred_element_type=jnp.float32
             )
-            for s in range(8):
+            for s in range(16):
                 lbuf[pl.ds(pl.multiple_of((a + s) * PITCH, 8), 128)] = pick(full, 128 * s)
 
     odd = zlo % 2
@@ -323,12 +323,12 @@
 
     acc[...] = jnp.zeros_like(acc)
 
-    @pl.loop(0, 64, step=16)
+    @pl.loop(0, 64, step=32)
     def _(d):
         right = jnp.concatenate(
             [lbuf[pl.ds(q * 64 + d + s, 64, stride=PITCH)].astype(jnp.bfloat16)
-             for s in range(16) for q in range(2)], axis=0)
-        tiles = [rbuf[d + s] for s in range(16)]
+             for s in range(32) for q in range(2)], axis=0)
+        tiles = [rbuf[d + s] for s in range(32)]
         left = jnp.concatenate(
             [jnp.concatenate([t[:, 128 * p : 128 * p + 128] for t in tiles], axis=1) for p in range(4)],
             axis=0)

time: 73.1 us -> 71.2 us (0.974)
  Pallas kernels: 70.9 us -> 69 us
    pallas_call x1, Pallas kernels: 70.9 us -> 69 us  [on_device(): pl.pallas_call(schur_kernel, out_shape=jax.ShapeDtypeStruct((per_row, PAN...]
where the time goes in v6:
time: 71.2 us; the launch traced here: 71 us
  Pallas kernels  69 us (97%)
  local copies, waits for them, and re-layouts  1.37 us (2%)
    pallas_call x1, Pallas kernels, on_device(): pl.pallas_call(schur_kernel, out_shape=jax.ShapeDtypeStruct((per_row, PAN...  69 us

profile of v6, /device:TPU:1, one launch (start us, length us, event | category | flops | bytes accessed | tf_op | source)
XLA Modules:
  0.0 71.0 jit_solution(17797516668008469667)
XLA Ops:
  0.6 69.0 %schur.1 = f32[2,32]{1,0:T(2,128)} custom-call(bf16[16,256,256]{2,1,0:T(8,128)(2,1)} %blocks.1, bf16[64,512]{1,0:T(8,128)(2,1)} %xt.1, bf16[64,512]{1,0:T(8,128)(2,1)} %wt.1, s32[1,128]{1,0:T(1,128)} %bitcast.1), custom_call_target="tpu_custom_call" | custom-call | tf_op jit(solution)/shard_map/schur/pallas_call | solution.py:425
  69.6 1.4 %fusion = (f32[2,16]{1,0:T(2,128)}, f32[2,16]{1,0:T(2,128)}) fusion(f32[2,32]{1,0:T(2,128)} %schur.1), kind=kLoop, calls=%fused_computation | loop fusion | bytes 512 | tf_op jit(solution)/shard_map/slice | solution.py:460
